TPU v7x, 128 devices: a whole 4x4x4 slice. The times are simulated.
128 devices in a mesh: px: 16 (over x_lo, y, core), py: 8 (over z, x_hi).
Axes of the slice: x: 4 (x_hi: 2, x_lo: 2; x = x_hi * 2 + x_lo), y: 4, z: 4, core: 2. Of those that a mesh axis runs over, the one named last changes fastest.
Arguments:
- field: float32 [1, 48, 128, 128, 256], P(None, None, 'px', 'py'), may hold values from -6 to 6
- spectral_weight: float32 [2, 32, 32, 32, 2304], P(None, 'py', None, 'px'), may hold values from -6 to 6
- pointwise_weight: float32 [48, 48], replicated, may hold values from -0.875 to 0.875
- channel_bias: float32 [48], replicated, may hold values from -3 to 3
Outputs:
- layer_out: float32 [1, 48, 128, 128, 256], P(None, None, 'px', 'py')
All inputs are finite; a program needn't handle non-finite values.
Results may differ from a plain program's by a relative error of at most 0.000065.
Values sent between devices are 32-bit elements; how exact they have to be, the bound alone decides.
A program may use at most 128 MiB of HBM per device.

v0:
```python
import math

import jax
import jax.numpy as jnp
from jax import lax
from jax.sharding import PartitionSpec as P


def tables(modes, length, signed):
    index = jnp.arange(length, dtype=jnp.int32)
    number = jnp.arange(modes, dtype=jnp.int32)
    if signed:
        number = jnp.where(number < modes // 2, number, number - modes)
    product = jnp.mod(index[:, None] * number[None, :], length)
    angle = product.astype(jnp.float32) * (2.0 * math.pi / length)
    return (jnp.cos(angle), jnp.sin(angle))


def shards(field, spectral_weight, pointwise_weight, channel_bias):
    precise = lax.Precision.HIGHEST
    batch, channels, x_local, y_local, z_length = field.shape
    x_groups = lax.axis_size("px")
    y_groups = lax.axis_size("py")
    x_length = x_local * x_groups
    y_length = y_local * y_groups
    x_share = spectral_weight.shape[1]
    modes = spectral_weight.shape[2]
    z_share = spectral_weight.shape[3]
    z_cos, z_sin = tables(modes, z_length, False)
    x_cos, x_sin = tables(modes, x_length, True)
    y_cos, y_sin = tables(modes, y_length, True)
    cos_groups = z_cos.reshape(z_length, x_groups, z_share)
    sin_groups = z_sin.reshape(z_length, x_groups, z_share)
    z_real = jnp.einsum("bcxyz,zgk->bxygkc", field, cos_groups, precision=precise)
    z_imag = -jnp.einsum("bcxyz,zgk->bxygkc", field, sin_groups, precision=precise)
    packed = jnp.stack([z_real, z_imag], axis=4).reshape(
        batch, x_local, y_local, x_groups, 2 * z_share * channels
    )
    moved = lax.all_to_all(packed, "px", split_axis=3, concat_axis=1, tiled=True)
    moved = moved.reshape(batch, x_length, y_local, 2, z_share, channels)
    v_real = moved[:, :, :, 0]
    v_imag = moved[:, :, :, 1]
    x_real = jnp.einsum("bxykc,xi->byikc", v_real, x_cos, precision=precise) + jnp.einsum(
        "bxykc,xi->byikc", v_imag, x_sin, precision=precise
    )
    x_imag = jnp.einsum("bxykc,xi->byikc", v_imag, x_cos, precision=precise) - jnp.einsum(
        "bxykc,xi->byikc", v_real, x_sin, precision=precise
    )
    grouped_real = x_real.reshape(batch, y_local, y_groups, x_share, z_share, channels)
    grouped_imag = x_imag.reshape(batch, y_local, y_groups, x_share, z_share, channels)
    packed_x = jnp.stack([grouped_real, grouped_imag], axis=4).reshape(
        batch, y_local, y_groups, x_share * 2 * z_share * channels
    )
    moved_x = lax.all_to_all(packed_x, "py", split_axis=2, concat_axis=1, tiled=True)
    moved_x = moved_x.reshape(batch, y_length, x_share, 2, z_share, channels)
    w_real = moved_x[:, :, :, 0]
    w_imag = moved_x[:, :, :, 1]
    y_real = jnp.einsum("byikc,yj->bijkc", w_real, y_cos, precision=precise) + jnp.einsum(
        "byikc,yj->bijkc", w_imag, y_sin, precision=precise
    )
    y_imag = jnp.einsum("byikc,yj->bijkc", w_imag, y_cos, precision=precise) - jnp.einsum(
        "byikc,yj->bijkc", w_real, y_sin, precision=precise
    )
    weights = spectral_weight.reshape(2, x_share, modes, z_share, channels, channels)
    h_real = jnp.einsum("bijkc,ijkco->bijko", y_real, weights[0], precision=precise) - jnp.einsum(
        "bijkc,ijkco->bijko", y_imag, weights[1], precision=precise
    )
    h_imag = jnp.einsum("bijkc,ijkco->bijko", y_real, weights[1], precision=precise) + jnp.einsum(
        "bijkc,ijkco->bijko", y_imag, weights[0], precision=precise
    )
    q_real = jnp.einsum("bijko,yj->byiko", h_real, y_cos, precision=precise) - jnp.einsum(
        "bijko,yj->byiko", h_imag, y_sin, precision=precise
    )
    q_imag = jnp.einsum("bijko,yj->byiko", h_real, y_sin, precision=precise) + jnp.einsum(
        "bijko,yj->byiko", h_imag, y_cos, precision=precise
    )
    packed_y = jnp.stack([q_real, q_imag], axis=3).reshape(
        batch, y_length, 1, x_share * 2 * z_share * channels
    )
    back_y = lax.all_to_all(packed_y, "py", split_axis=1, concat_axis=2, tiled=True)
    back_y = back_y.reshape(batch, y_local, modes, 2, z_share, channels)
    r_real = back_y[:, :, :, 0]
    r_imag = back_y[:, :, :, 1]
    p_real = jnp.einsum("byiko,xi->bxyko", r_real, x_cos, precision=precise) - jnp.einsum(
        "byiko,xi->bxyko", r_imag, x_sin, precision=precise
    )
    p_imag = jnp.einsum("byiko,xi->bxyko", r_real, x_sin, precision=precise) + jnp.einsum(
        "byiko,xi->bxyko", r_imag, x_cos, precision=precise
    )
    packed_back = jnp.stack([p_real, p_imag], axis=3).reshape(
        batch, x_length, y_local, 1, 2 * z_share * channels
    )
    back_x = lax.all_to_all(packed_back, "px", split_axis=1, concat_axis=3, tiled=True)
    back_x = back_x.reshape(batch, x_local, y_local, x_groups, 2, z_share, channels)
    factor = jnp.where(jnp.arange(modes) == 0, 1.0, 2.0).astype(jnp.float32) / (
        x_length * y_length * z_length
    )
    inv_cos = (z_cos * factor[None, :]).reshape(z_length, x_groups, z_share)
    inv_sin = (z_sin * factor[None, :]).reshape(z_length, x_groups, z_share)
    spectral = jnp.einsum(
        "bxygko,zgk->boxyz", back_x[:, :, :, :, 0], inv_cos, precision=precise
    ) - jnp.einsum("bxygko,zgk->boxyz", back_x[:, :, :, :, 1], inv_sin, precision=precise)
    local_term = jnp.einsum("bcxyz,co->boxyz", field, pointwise_weight, precision=precise)
    total = spectral + local_term + channel_bias[None, :, None, None, None]
    return jax.nn.gelu(total, approximate=False)


def solution(mesh):
    in_specs = (P(None, None, "px", "py", None), P(None, "py", None, "px", None), P(), P())
    out_specs = P(None, None, "px", "py", None)
    return jax.shard_map(shards, mesh=mesh, in_specs=in_specs, out_specs=out_specs, check_vma=False)
```

profile of v0, /device:TPU:25, one launch (start us, length us, event | category | flops | bytes accessed | tf_op | source)
XLA Modules:
  0.0 285.7 jit_solution(11340280697742805434)
XLA Ops:
  0.0 16.2 %fusion.22 = f32[1,8,16,16,1,2,48]{6,3,2,1,5,4,0:T(8,128)S(1)} fusion(f32[48,8,16,256]{3,2,1,0:T(8,128)} %bitcast.248, s32[16,2]{0,1:T(2,128)S(1)} %multiply_add_fusion), kind=kOutput, calls=%fused_computation.35 | convolution fusion | flops 604094464 | bytes 7078016 | tf_op jit(solution)/shard_map/bcxyz,zgk->bxygkc/dot_general | solution.py:34
  16.2 13.0 %negate_bitcast_fusion = f32[1,8,16,16,1,2,48]{6,3,2,1,5,4,0:T(8,128)S(1)} fusion(f32[48,8,16,256]{3,2,1,0:T(8,128)S(1)} %bitcast.249, s32[16,2]{0,1:T(2,128)S(1)} %multiply_add_fusion), kind=kOutput, calls=%fused_computation.34 | convolution fusion | flops 604291072 | bytes 7078016 | tf_op jit(solution)/shard_map/bcxyz,zgk->bxygkc/dot_general | solution.py:35
  29.6 5.8 %copy.95 = f32[1,8,16,16,2,2,48]{6,5,4,2,1,3,0:T(2,128)} copy(f32[1,8,16,16,2,2,48]{6,3,2,1,5,4,0:T(8,128)S(1)} %pad_maximum_fusion) | data formatting | bytes 3145728 | tf_op jit(solution)/shard_map/reshape | solution.py:36
  35.3 6.0 %reshape.340 = f32[1,8,16,16,192]{4,2,1,0,3:T(8,128)} reshape(f32[1,8,16,16,2,2,48]{6,5,4,2,1,3,0:T(2,128)} %copy.95) | data formatting | bytes 3145728 | tf_op jit(solution)/shard_map/reshape | solution.py:36
  41.4 5.9 %all-to-all-start = ((f32[1,8,16,16,192]{4,2,1,0,3:T(8,128)}), f32[1,8,16,16,192]{4,2,1,0,3:T(8,128)S(1)}, u32[]{:S(2)}, u32[]{:S(2)}) async-start(f32[1,8,16,16,192]{4,2,1,0,3:T(8,128)} %reshape.340), calls=%async_computation | async-start | bytes 4194304 | tf_op jit(solution)/shard_map/all_to_all | solution.py:39
  47.3 29.5 %all-to-all-done = f32[1,8,16,16,192]{4,2,1,0,3:T(8,128)S(1)} async-done(((f32[1,8,16,16,192]{4,2,1,0,3:T(8,128)}), f32[1,8,16,16,192]{4,2,1,0,3:T(8,128)S(1)}, u32[]{:S(2)}, u32[]{:S(2)}) %all-to-all-start) | async-done | bytes 1572896 | tf_op jit(solution)/shard_map/all_to_all | solution.py:39
  76.8 5.1 %reshape.306 = f32[1,128,16,2,2,48]{5,4,3,2,1,0:T(2,128)} reshape(f32[1,16,8,16,1,192]{5,3,2,1,4,0:T(8,128)S(1)} %bitcast.253) | data formatting | bytes 3145728 | tf_op jit(solution)/shard_map/reshape | solution.py:40
  82.0 5.5 %fusion.201 = (f32[1,128,16,1,2,48]{5,4,3,2,1,0:T(2,128)}, f32[1,128,16,1,2,48]{5,4,3,2,1,0:T(2,128)S(1)}) fusion(f32[1,128,16,2,2,48]{5,4,3,2,1,0:T(2,128)} %reshape.306), kind=kLoop, calls=%fused_computation.214 | loop fusion | bytes 3145728 | tf_op jit(solution)/shard_map/slice | solution.py:41
  109.5 7.4 %all-to-all-start.1 = ((f32[1,16,8,768]{3,1,0,2:T(8,128)}), f32[1,16,8,768]{3,1,0,2:T(8,128)S(1)}, u32[]{:S(2)}, u32[]{:S(2)}) async-start(f32[1,16,8,768]{3,1,0,2:T(8,128)} %copy.64), calls=%async_computation.1 | async-start | bytes 786432 | tf_op jit(solution)/shard_map/all_to_all | solution.py:54
  117.0 5.4 %fusion.199 = (f32[1,4,32,2,2304]{4,3,2,1,0:T(2,128)}, f32[1,4,32,2,2304]{4,3,2,1,0:T(2,128)S(1)}) fusion(f32[2,4,32,2,2304]{4,3,2,1,0:T(2,128)} %param.5), kind=kLoop, calls=%fused_computation.212 | loop fusion | bytes 9437184 | tf_op jit(solution)/shard_map/slice | solution.py:65
  122.4 7.1 %squeeze.4 = f32[4,32,2,48,48]{4,3,2,1,0:T(8,128)} reshape(f32[1,4,32,2,2304]{4,3,2,1,0:T(2,128)} %get-tuple-element.5) | data formatting | bytes 4718592 | tf_op jit(solution)/shard_map/squeeze | solution.py:65
  129.5 5.5 %squeeze.5 = f32[4,32,2,48,48]{4,3,2,1,0:T(8,128)} reshape(f32[1,4,32,2,2304]{4,3,2,1,0:T(2,128)S(1)} %get-tuple-element.6) | data formatting | bytes 4718592 | tf_op jit(solution)/shard_map/squeeze | solution.py:66
  141.0 7.7 %fusion.47 = f32[4,32,2,1,48]{4,3,2,1,0:T(1,128)S(1)} fusion(f32[4,32,2,48,48]{4,3,2,1,0:T(8,128)} %squeeze.4, f32[4,32,2,48,1]{3,1,2,0,4:T(8,128)S(1)} %fusion.31), kind=kOutput, calls=%fused_computation.71 | convolution fusion | flops 7077888 | bytes 2457600 | tf_op jit(solution)/shard_map/bijkc,ijkco->bijko/dot_general | solution.py:68
  148.7 7.8 %fusion.53 = f32[4,32,2,1,48]{4,3,2,1,0:T(1,128)S(1)} fusion(f32[4,32,2,48,48]{4,3,2,1,0:T(8,128)} %squeeze.4, f32[4,32,2,48,1]{3,1,2,0,4:T(8,128)S(1)} %fusion.32), kind=kOutput, calls=%fused_computation.77 | convolution fusion | flops 7077888 | bytes 2457600 | tf_op jit(solution)/shard_map/bijkc,ijkco->bijko/dot_general | solution.py:65
  156.5 5.4 %fusion.51 = f32[4,32,2,1,48]{4,3,2,1,0:T(1,128)S(1)} fusion(f32[4,32,2,48,48]{4,3,2,1,0:T(8,128)S(1)} %bitcast.247, f32[4,32,2,48,1]{3,1,2,0,4:T(8,128)S(1)} %fusion.32), kind=kOutput, calls=%fused_computation.75 | convolution fusion | flops 7077888 | bytes 2457600 | tf_op jit(solution)/shard_map/bijkc,ijkco->bijko/dot_general | solution.py:68
  161.9 5.4 %fusion.49 = f32[4,32,2,1,48]{4,3,2,1,0:T(1,128)S(1)} fusion(f32[4,32,2,48,48]{4,3,2,1,0:T(8,128)S(1)} %bitcast.247, f32[4,32,2,48,1]{3,1,2,0,4:T(8,128)S(1)} %fusion.31), kind=kOutput, calls=%fused_computation.73 | convolution fusion | flops 7077888 | bytes 2457600 | tf_op jit(solution)/shard_map/bijkc,ijkco->bijko/dot_general | solution.py:65
  170.3 15.6 %all_to_all.60 = f32[1,128,1,768]{3,2,0,1:T(1,128)S(1)} all-to-all(f32[1,128,1,768]{3,2,0,1:T(1,128)S(1)} %copy.68), channel_id=1, replica_groups=mesh['px'=16,'py'=8] {'py'}, dimensions={1} | all-to-all | bytes 786432 | tf_op jit(solution)/shard_map/all_to_all | solution.py:80
  198.1 6.3 %all-to-all-start.3 = ((f32[1,128,16,1,192]{4,3,2,0,1:T(1,128)}), f32[1,128,16,1,192]{4,3,2,0,1:T(1,128)}, u32[]{:S(2)}, u32[]{:S(2)}) async-start(f32[1,128,16,1,192]{4,3,2,0,1:T(1,128)} %copy.73), calls=%async_computation.3 | async-start | bytes 4194304 | tf_op jit(solution)/shard_map/all_to_all | solution.py:93
  204.4 29.6 %all-to-all-done.3 = f32[1,128,16,1,192]{4,3,2,0,1:T(1,128)} async-done(((f32[1,128,16,1,192]{4,3,2,0,1:T(1,128)}), f32[1,128,16,1,192]{4,3,2,0,1:T(1,128)}, u32[]{:S(2)}, u32[]{:S(2)}) %all-to-all-start.3) | async-done | bytes 1572896 | tf_op jit(solution)/shard_map/all_to_all | solution.py:93
  235.7 5.3 %reshape.341 = f32[1,8,16,16,2,2,48]{6,5,4,2,1,3,0:T(2,128)} reshape(f32[1,8,16,16,1,192]{5,2,1,3,4,0:T(8,128)S(1)} %bitcast.254) | data formatting | bytes 3145728 | tf_op jit(solution)/shard_map/reshape | solution.py:94
  245.2 5.6 %fusion.21 = f32[256,8,16,48,1]{0,3,4,2,1:T(8,128)S(1)} fusion(f32[1,8,16,16,1,2,48]{6,5,4,2,1,3,0:T(2,128)S(1)} %get-tuple-element.7, f32[16,2]{0,1:T(2,128)S(1)} %fusion.118, s32[16,2]{0,1:T(2,128)S(1)} %multiply_add_fusion), kind=kOutput, calls=%fused_computation.33 | convolution fusion | flops 604102656 | bytes 7078144 | tf_op jit(solution)/shard_map/bxygko,zgk->boxyz/dot_general | solution.py:100
  250.8 6.0 %fusion.20 = f32[256,8,16,48,1]{0,3,4,2,1:T(8,128)S(1)} fusion(f32[1,8,16,16,1,2,48]{6,5,4,2,1,3,0:T(2,128)S(1)} %get-tuple-element.8, f32[16,2]{0,1:T(2,128)S(1)} %fusion.118, s32[16,2]{0,1:T(2,128)S(1)} %multiply_add_fusion), kind=kOutput, calls=%fused_computation.31 | convolution fusion | flops 604102656 | bytes 7078144 | tf_op jit(solution)/shard_map/bxygko,zgk->boxyz/dot_general | solution.py:102
  256.9 22.3 %fusion.1 = f32[1,48,8,16,256]{4,1,3,2,0:T(8,128)S(1)} fusion(f32[256,8,16,48,1]{0,3,4,2,1:T(8,128)S(1)} %fusion.20, f32[256,8,16,48,1]{0,3,4,2,1:T(8,128)S(1)} %fusion.21, f32[48]{0:T(128)S(1)} %copy-done.2, f32[48,8,16,256]{3,2,1,0:T(8,128)S(1)} %bitcast.252, f32[48,48]{1,0:T(8,128)S(1)} %copy-done), kind=kOutput, calls=%fused_computation.2 | convolution fusion | flops 1011351552 | bytes 25175232 | tf_op jit(solution)/shard_map/bcxyz,co->boxyz/dot_general | solution.py:103
  279.2 6.3 %copy.79 = f32[1,48,8,16,256]{4,3,2,1,0:T(8,128)} copy(f32[1,48,8,16,256]{4,1,3,2,0:T(8,128)S(1)} %fusion.1) | data formatting | bytes 12582912 | tf_op jit(solution)/shard_map/mul | solution.py:105
  (60 shorter events, 49.3 us)
Async XLA Ops:
  0.0 256.8 %copy-start = (f32[48,48]{1,0:T(8,128)S(1)}, f32[48,48]{1,0:T(8,128)}, u32[]{:S(2)}) copy-start(f32[48,48]{1,0:T(8,128)} %param.6) | copy-start | bytes 27652
  0.0 16.2 %copy-start.1 = (f32[1,48,8,16,256]{4,3,2,1,0:T(8,128)S(1)}, f32[1,48,8,16,256]{4,3,2,1,0:T(8,128)}, u32[]{:S(2)}) copy-start(f32[1,48,8,16,256]{4,3,2,1,0:T(8,128)} %param.4) | copy-start | bytes 18874372
  41.4 35.5 %all-to-all-start = ((f32[1,8,16,16,192]{4,2,1,0,3:T(8,128)}), f32[1,8,16,16,192]{4,2,1,0,3:T(8,128)S(1)}, u32[]{:S(2)}, u32[]{:S(2)}) async-start(f32[1,8,16,16,192]{4,2,1,0,3:T(8,128)} %reshape.340), calls=%async_computation | async-start | bytes 4194304 | tf_op jit(solution)/shard_map/all_to_all | solution.py:39
  109.5 25.4 %all-to-all-start.1 = ((f32[1,16,8,768]{3,1,0,2:T(8,128)}), f32[1,16,8,768]{3,1,0,2:T(8,128)S(1)}, u32[]{:S(2)}, u32[]{:S(2)}) async-start(f32[1,16,8,768]{3,1,0,2:T(8,128)} %copy.64), calls=%async_computation.1 | async-start | bytes 786432 | tf_op jit(solution)/shard_map/all_to_all | solution.py:54
  140.1 16.3 %slice-start = ((s8[6291456]{0:T(1024)(128)(4,1)}), s8[4194304]{0:T(1024)(128)(4,1)S(1)}, s32[]{:S(2)}) async-start(s8[6291456]{0:T(1024)(128)(4,1)} %bitcast.246), calls=%async_computation.4 | async-start | bytes 8388608
  141.0 15.5 %slice-start.1 = ((s8[6291456]{0:T(1024)(128)(4,1)}), s8[2097152]{0:T(1024)(128)(4,1)S(1)}, s32[]{:S(2)}) async-start(s8[6291456]{0:T(1024)(128)(4,1)} %bitcast.246), calls=%async_computation.5 | async-start | bytes 4194304
  198.1 35.9 %all-to-all-start.3 = ((f32[1,128,16,1,192]{4,3,2,0,1:T(1,128)}), f32[1,128,16,1,192]{4,3,2,0,1:T(1,128)}, u32[]{:S(2)}, u32[]{:S(2)}) async-start(f32[1,128,16,1,192]{4,3,2,0,1:T(1,128)} %copy.73), calls=%async_computation.3 | async-start | bytes 4194304 | tf_op jit(solution)/shard_map/all_to_all | solution.py:93
  245.2 11.6 %slice-start.2 = ((s8[6291456]{0:T(1024)(128)(4,1)}), s8[4194304]{0:T(1024)(128)(4,1)S(1)}, s32[]{:S(2)}) async-start(s8[6291456]{0:T(1024)(128)(4,1)} %bitcast.250), calls=%async_computation.6 | async-start | bytes 8388608
  250.8 6.1 %slice-start.3 = ((s8[6291456]{0:T(1024)(128)(4,1)}), s8[2097152]{0:T(1024)(128)(4,1)S(1)}, s32[]{:S(2)}) async-start(s8[6291456]{0:T(1024)(128)(4,1)} %bitcast.250), calls=%async_computation.7 | async-start | bytes 4194304
  250.8 6.0 %copy-start.2 = (f32[48]{0:T(128)S(1)}, f32[48]{0:T(128)}, u32[]{:S(2)}) copy-start(f32[48]{0:T(128)} %param.7) | copy-start | bytes 580
where the time goes:
time: 291 us; the launch traced here: 286 us
  matrix products  114 us (39%)
  local copies, waits for them, and re-layouts  75.4 us (26%)
  waiting for transfers between devices  59.1 us (20%)
  starting transfers between devices  19.7 us (7%)
  blocking collectives  15.6 us (5%)
    all_to_all x1, waiting for transfers between devices, shards(): lax.all_to_all(packed_back, 'px', split_axis=1, concat_axis=3, tiled=True)  29.6 us
    all_to_all x1, waiting for transfers between devices, shards(): lax.all_to_all(packed, 'px', split_axis=3, concat_axis=1, tiled=True)  29.5 us
    dot_general x1, matrix products, shards(): jnp.einsum('bcxyz,co->boxyz', field, pointwise_weight, precision=precise)  22.3 us
    dot_general x1, matrix products, shards(): jnp.einsum('bcxyz,zgk->bxygkc', field, cos_groups, precision=precise)  16.2 us
    all_to_all x1, blocking collectives, shards(): lax.all_to_all(packed_y, 'py', split_axis=1, concat_axis=2, tiled=True)  15.6 us
    dot_general x1, matrix products, shards(): jnp.einsum('bcxyz,zgk->bxygkc', field, sin_groups, precision=precise)  13 us
    reshape x2, local copies, waits for them, and re-layouts, shards(): jnp.stack([z_real, z_imag], axis=4)  11.8 us
    dot_general x1, matrix products, shards(): jnp.einsum('bijkc,ijkco->bijko', y_real, weights[0], precision=precise)  7.75 us
  transfers between devices with their start and end apart: 3, of which 2 were waited for; matrix products, arithmetic and copies ran while one was open for 6% of the time, Pallas kernels for 0%

commit v1 on v0

v1 whole, which is shorter than its diff:
```python
import functools
import math

import jax
import jax.numpy as jnp
import ml_dtypes
import numpy as np
from jax import lax
from jax.experimental import pallas as pl
from jax.experimental.pallas import tpu as pltpu
from jax.sharding import PartitionSpec as P

MESH = pl.DeviceIdType.MESH
BF = jnp.bfloat16
F32 = jnp.float32
ANY = pl.BlockSpec(memory_space=pl.ANY)
VMEM = pl.BlockSpec(memory_space=pltpu.VMEM)

NX, NY, NZ, MODES, CH, G, H = 128, 128, 256, 32, 48, 16, 8
CT = CH // 16


def halves(table):
    high = table.astype(ml_dtypes.bfloat16)
    low = (table - high.astype(np.float64)).astype(ml_dtypes.bfloat16)
    return high, low


def signed(modes):
    number = np.arange(modes)
    return np.where(number < modes // 2, number, number - modes)


def angles(position, mode, length):
    return 2.0 * math.pi * ((position[:, None] * mode[None, :]) % length) / length


def lane_parts():
    lane = np.arange(128)
    return lane // 64, (lane // 32) % 2, (lane // 16) % 2, lane % 16


@functools.cache
def constants():
    ri, y2, k2, low = lane_parts()
    k = 2 * low + k2
    a = angles(np.arange(NZ), k, NZ)
    wave = np.where(ri[None, :] == 0, np.cos(a), -np.sin(a))
    forward = np.concatenate([wave * (y2 == 0), wave * (y2 == 1)], axis=0)
    tz = np.concatenate(halves(forward), axis=1)
    gain = np.where(k == 0, 1.0, 2.0) / (NX * NY * NZ)
    eh, el = halves((forward * gain).T)
    ez = np.concatenate([eh, eh], axis=0)
    f = signed(MODES)
    ax = angles(np.arange(NX), f, NX)
    ch, cl = halves(np.concatenate([np.cos(ax).T, np.sin(ax).T], axis=0))
    lx = np.concatenate(
        [np.concatenate([ch, ch], axis=1), np.concatenate([cl, np.zeros_like(cl)], axis=1)], axis=0
    )
    ch, cl = halves(np.concatenate([np.cos(ax), np.sin(ax)], axis=0))
    lix = np.concatenate([ch, ch, cl], axis=1)
    y = np.arange(NY).reshape(H, 2, 8)
    parts = [y[:, h].reshape(-1) for h in range(2)]
    ay = [angles(p, f, NY) for p in parts]
    rows = np.concatenate([t for q in ay for t in (np.cos(q).T, np.sin(q).T)], axis=0)
    ch, cl = halves(rows)
    ly = np.concatenate(
        [np.concatenate([ch, ch], axis=1), np.concatenate([cl, np.zeros_like(cl)], axis=1)], axis=0
    )
    rows = np.concatenate([np.cos(ay[0]), np.cos(ay[1]), np.sin(ay[0]), np.sin(ay[1])], axis=0)
    ch, cl = halves(rows)
    liy = np.concatenate([ch, ch, cl], axis=1)
    spread = np.zeros((128, 2, 2, 2, 8, CH))
    for half in range(2):
        for r in range(2):
            for q in range(2):
                for c in range(8):
                    spread[r * 64 + 32 + q * 16 + half * 8 + c, half, r, q, c, :] = 1.0
    spread = spread.reshape(128, -1)
    spread = np.concatenate([spread, spread], axis=0).astype(ml_dtypes.bfloat16)
    gather = np.zeros((2, 2, 8, CH, CT, 128))
    for q in range(2):
        for r in range(2):
            for o in range(CH):
                for h in range(2):
                    gather[q, r, :, o, o // 16, r * 64 + h * 32 + q * 16 + o % 16] = 1.0
    gather = gather.reshape(2 * 2 * 8 * CH, CT * 128).astype(ml_dtypes.bfloat16)
    return tz, lx, ly, spread, gather, liy, lix, ez, el


def split(value):
    high = value.astype(BF)
    return high, (value - high.astype(F32)).astype(BF)


def dot(a, b):
    return jnp.dot(a, b, preferred_element_type=F32)


def lanes16(tiles, lane):
    tiles = list(tiles)
    for bit in range(4):
        step = 1 << bit
        keep = (lane & step) == 0
        for index in range(16):
            if index & step:
                continue
            a, b = tiles[index], tiles[index | step]
            tiles[index] = jnp.where(keep, a, pltpu.roll(b, step, 1))
            tiles[index | step] = jnp.where(keep, pltpu.roll(a, 128 - step, 1), b)
    return tiles


def spectral_kernel(
    field, weight, spread, gather, tz, lx, ly, liy, lix, out,
    f_in, w_in, e_in, r_in, send1, recv1, send2, recv2, send3, recv3, send4, v_exp, h_acc, h_all,
    f_sem, w_sem, c_sem, s1, r1, s2, r2, s3, r3, s4, r4, o_sem,
):
    me, my = lax.axis_index("px"), lax.axis_index("py")

    def field_copy(t):
        return pltpu.make_async_copy(field.at[pl.ds(t * 16, 16)], f_in.at[pl.ds(t * 16, 16)], f_sem.at[t])

    def weight_copy(r, q):
        return pltpu.make_async_copy(weight.at[r, :, :, q, :], w_in.at[r, q], w_sem.at[r, q])

    const_copies = [
        pltpu.make_async_copy(spread, e_in, c_sem.at[0]),
        pltpu.make_async_copy(gather, r_in, c_sem.at[1]),
    ]
    for t in range(CT):
        field_copy(t).start()
    for copy in const_copies:
        copy.start()
    for r in range(2):
        for q in range(2):
            weight_copy(r, q).start()

    barrier = pltpu.get_barrier_semaphore()

    def greet_x(d, c):
        pl.semaphore_signal(barrier, inc=1, device_id=(lax.rem(me + d, G), my), device_id_type=MESH)
        return c

    def greet_y(d, c):
        pl.semaphore_signal(barrier, inc=1, device_id=(me, lax.rem(my + d, H)), device_id_type=MESH)
        return c

    lax.fori_loop(1, G, greet_x, 0)
    lax.fori_loop(1, H, greet_y, 0)
    pl.semaphore_wait(barrier, G + H - 2)

    def copy1(t, target, source):
        return pltpu.make_async_remote_copy(
            send1.at[t, target], recv1.at[t, pl.ds(source * 64, 64)], s1.at[t, target], r1.at[t, source],
            device_id=(target, my), device_id_type=MESH)

    def copy2(t, target, source):
        return pltpu.make_async_remote_copy(
            send2.at[t, pl.ds(target * 32, 32)], recv2.at[t, pl.ds(source * 32, 32)], s2.at[t, target],
            r2.at[t, source], device_id=(me, target), device_id_type=MESH)

    def copy3(t, target, source):
        return pltpu.make_async_remote_copy(
            send3.at[t, target], recv3.at[t, pl.ds(source * 32, 32)], s3.at[t, target], r3.at[t, source],
            device_id=(me, target), device_id_type=MESH)

    def copy4(t, target, source):
        return pltpu.make_async_remote_copy(
            send4.at[t, pl.ds(target * 64, 64)], out.at[t, source], s4.at[t, target], r4.at[t, source],
            device_id=(target, my), device_id_type=MESH)

    def send_all(copy, t, index, count):
        def body(d, c):
            copy(t, lax.rem(index + d, count), index).start()
            return c
        lax.fori_loop(1, count, body, 0)

    def wait_recv(copy, t, index, count):
        def body(d, c):
            peer = lax.rem(index + count - d, count)
            copy(t, peer, peer).wait_recv()
            return c
        lax.fori_loop(1, count, body, 0)

    def wait_send(copy, t, index, count):
        def body(d, c):
            copy(t, lax.rem(index + d, count), index).wait_send()
            return c
        lax.fori_loop(1, count, body, 0)

    lane = lax.broadcasted_iota(jnp.int32, (8, 128), 1)
    wide = lax.broadcasted_iota(jnp.int32, (1, 128), 1)
    sign = jnp.where(wide < 64, 1.0, -1.0).astype(F32)
    first = (wide & 32) == 0

    for t in range(CT):
        field_copy(t).wait()

        def z_step(xq, c, t=t):
            block = f_in[t * 16:(t + 1) * 16, pl.ds(xq * 4, 4)]
            rows = jnp.concatenate(
                [block[:, :, :8].reshape(512, NZ), block[:, :, 8:].reshape(512, NZ)], axis=1)
            high, low = split(rows)
            both = dot(high, tz[...])
            z = both[:, :128] + both[:, 128:] + dot(low, tz[:, :128])
            z = z.reshape(16, 4, 8, 128)
            for x in range(4):
                tiles = lanes16([z[c16, x] for c16 in range(16)], lane)
                for g in range(16):
                    send1[t, g, pl.ds(xq * 32 + x * 8, 8), :] = tiles[g]
            return c

        lax.fori_loop(0, 2, z_step, 0)
        send_all(copy1, t, me, G)
        recv1[t, pl.ds(me * 64, 64), :] = send1[t, me]

    for t in range(CT):
        wait_recv(copy1, t, me, G)
        for pair in range(4):
            data = jnp.concatenate(
                [recv1[t, pl.ds(2 * pair + h, 128, stride=8), :] for h in range(2)], axis=1)
            prod = dot(lx[...], jnp.concatenate(split(data), axis=0))
            prod = prod[:64] + prod[64:]
            for h in range(2):
                piece = prod[:, h * 128:(h + 1) * 128]
                send2[t, pl.ds(2 * pair + h, 32, stride=8), :] = piece[:32] + sign * pltpu.roll(piece[32:], 64, 1)
        send_all(copy2, t, my, H)
        recv2[t, pl.ds(my * 32, 32), :] = send2[t, pl.ds(my * 32, 32), :]

    for copy in const_copies:
        copy.wait()
    for t in range(CT):
        wait_recv(copy2, t, my, H)
        data = recv2[t].reshape(H, 4, 8, 128)
        data = jnp.concatenate([data[:, i].reshape(64, 128) for i in range(4)], axis=1)
        prod = dot(ly[...], jnp.concatenate(split(data), axis=0))
        prod = prod[:128] + prod[128:]
        rows = []
        for i in range(4):
            piece = prod[:, i * 128:(i + 1) * 128]
            u = jnp.where(first, piece[:32], piece[64:96])
            w = jnp.where(first, piece[32:64], piece[96:])
            v = u + sign * pltpu.roll(w, 64, 1)
            rows.append(v + pltpu.roll(v, 32, 1))
        v = jnp.concatenate(rows, axis=0)
        v_exp[t] = dot(jnp.concatenate(split(v), axis=1), e_in[...])

    for r in range(2):
        for q in range(2):
            weight_copy(r, q).wait()

    def mix(i, c):
        at = pl.ds(pl.multiple_of(i * 32, 32), 32)
        for q in range(2):
            for part in range(3):
                real = jnp.zeros((32, 128), F32)
                imag = jnp.zeros((32, 128), F32)
                for b in range(6):
                    base = (b % 2) * 4 * 384 + q * 384 + part * 128
                    vr = v_exp[b // 2, at, base:base + 128]
                    vi = v_exp[b // 2, at, base + 768:base + 768 + 128]
                    w0 = w_in[0, q, i, :, b * 384 + part * 128:b * 384 + part * 128 + 128]
                    w1 = w_in[1, q, i, :, b * 384 + part * 128:b * 384 + part * 128 + 128]
                    real += vr * w0 - vi * w1
                    imag += vr * w1 + vi * w0
                h_acc[at, q * 768 + part * 128:q * 768 + part * 128 + 128] = real
                h_acc[at, q * 768 + 384 + part * 128:q * 768 + 384 + part * 128 + 128] = imag
        return c

    lax.fori_loop(0, 4, mix, 0)
    high, low = split(h_acc[...])
    h_all[...] = dot(high, r_in[...]) + dot(low, r_in[...])

    for t in range(CT):
        data = jnp.concatenate(
            [h_all[i * 32:(i + 1) * 32, t * 128:(t + 1) * 128] for i in range(4)], axis=1)
        high, low = split(data)
        prod = dot(liy[...], jnp.concatenate([high, low, high], axis=0))
        for i in range(4):
            piece = prod[:, i * 128:(i + 1) * 128]
            a = jnp.where(first, piece[:64], piece[64:128])
            b = jnp.where(first, piece[128:192], piece[192:])
            q = a - sign * pltpu.roll(b, 64, 1)
            send3[t, :, i * 8:(i + 1) * 8, :] = q.reshape(H, 8, 128)
        send_all(copy3, t, my, H)
        recv3[t, pl.ds(my * 32, 32), :] = send3[t, my]

    for t in range(CT):
        wait_recv(copy3, t, my, H)
        for pair in range(4):
            data = jnp.concatenate(
                [recv3[t, pl.ds(2 * pair + h, 32, stride=8), :] for h in range(2)], axis=1)
            high, low = split(data)
            prod = dot(lix[...], jnp.concatenate([high, low, high], axis=0))
            for h in range(2):
                piece = prod[:, h * 128:(h + 1) * 128]
                send4[t, pl.ds(2 * pair + h, 128, stride=8), :] = piece[:128] - sign * pltpu.roll(piece[128:], 64, 1)
        send_all(copy4, t, me, G)
        pltpu.make_async_copy(send4.at[t, pl.ds(me * 64, 64)], out.at[t, me], o_sem.at[t]).start()

    for t in range(CT):
        wait_recv(copy4, t, me, G)
        pltpu.make_async_copy(send4.at[t, pl.ds(me * 64, 64)], out.at[t, me], o_sem.at[t]).wait()
        wait_send(copy1, t, me, G)
        wait_send(copy2, t, my, H)
        wait_send(copy3, t, my, H)
        wait_send(copy4, t, me, G)


def gelu(v):
    x = jnp.clip(v * math.sqrt(0.5), -3.832506856900711, 3.832506856900711)
    s = x * x
    top = jnp.full_like(s, 0.00022905065861350646)
    for a in (0.0034082910107109506, 0.050955695062380861, 0.18520832239976145, 1.128379143519084):
        top = top * s + a
    low = jnp.full_like(s, -1.1791602954361697e-7)
    for a in (0.000023547966471313185, 0.0010179625278914885, 0.014070470171167667, 0.11098505178285362,
              0.49746925110067538, 1.0):
        low = low * s + a
    return 0.5 * v * (1.0 + x * top / low)


def final_kernel(modes, field, point, bias, ez, el, out, a_high, a_low, shift):
    @pl.when(pl.program_id(0) == 0)
    def _():
        row = lax.broadcasted_iota(jnp.int32, (384, CH), 0)
        col = lax.broadcasted_iota(jnp.int32, (384, CH), 1)
        pick = (row // 8 == col)
        shift[...] = jnp.sum(jnp.where(pick, bias[...], 0.0), axis=1, keepdims=True) + jnp.zeros((384, 128), F32)
        picked = pick.astype(F32).astype(BF)
        r = lax.broadcasted_iota(jnp.int32, (384, 384), 0)
        c = lax.broadcasted_iota(jnp.int32, (384, 384), 1)
        same = (r % 8) == (c % 8)
        for piece, ref in zip(split(point[...]), (a_high, a_low)):
            wide = lax.dot_general(picked, piece, (((1,), (1,)), ((), ())), preferred_element_type=F32)
            full = lax.dot_general(wide.astype(BF), picked, (((1,), (1,)), ((), ())), preferred_element_type=F32)
            ref[...] = jnp.where(same, full, 0.0).astype(BF)

    lane = lax.broadcasted_iota(jnp.int32, (8, 128), 1)
    tiles = []
    for t in range(CT):
        tiles += lanes16([modes[t, s] for s in range(G)], lane)
    high, low = split(jnp.concatenate(tiles, axis=0))
    spectral = dot(jnp.concatenate([high, low], axis=1), ez[...]) + dot(high, el[...])
    for h in range(2):
        data = field[:, 0, h * 8:(h + 1) * 8, :].reshape(384, NZ)
        high, low = split(data)
        local = dot(a_high[...], high) + dot(a_low[...], high) + dot(a_high[...], low)
        total = spectral[:, h * NZ:(h + 1) * NZ] + local + shift[:, :1]
        out[:, 0, h * 8:(h + 1) * 8, :] = gelu(total).reshape(CH, 8, NZ)


def shards(field, spectral_weight, pointwise_weight, channel_bias):
    tz, lx, ly, spread, gather, liy, lix, ez, el = [jnp.asarray(c) for c in constants()]
    x_local = field.shape[2]
    field = field.reshape(field.shape[1:])
    scratch = [
        pltpu.VMEM((CH, 8, 16, NZ), F32),
        pltpu.VMEM((2, 2, 4, MODES, CH * CH), F32),
        pltpu.VMEM(spread.shape, BF),
        pltpu.VMEM(gather.shape, BF),
        pltpu.VMEM((CT, G, 64, 128), F32),
        pltpu.VMEM((CT, G * 64, 128), F32),
        pltpu.VMEM((CT, H * 32, 128), F32),
        pltpu.VMEM((CT, H * 32, 128), F32),
        pltpu.VMEM((CT, H, 32, 128), F32),
        pltpu.VMEM((CT, H * 32, 128), F32),
        pltpu.VMEM((CT, G * 64, 128), F32),
        pltpu.VMEM((CT, 128, 3072), F32),
        pltpu.VMEM((128, 1536), F32),
        pltpu.VMEM((128, 384), F32),
    ]
    dma = pltpu.SemaphoreType.DMA
    scratch += [dma((CT,)), dma((2, 2)), dma((2,))]
    scratch += [dma((CT, G)), dma((CT, G)), dma((CT, H)), dma((CT, H))]
    scratch += [dma((CT, H)), dma((CT, H)), dma((CT, G)), dma((CT, G)), dma((CT,))]
    modes = pl.pallas_call(
        spectral_kernel,
        out_shape=jax.ShapeDtypeStruct((CT, G, 64, 128), F32),
        in_specs=[ANY] * 4 + [VMEM] * 5,
        out_specs=ANY,
        scratch_shapes=scratch,
        compiler_params=pltpu.CompilerParams(
            collective_id=0, has_side_effects=True, vmem_limit_bytes=56 * 1024 * 1024),
        name="spectral",
    )(field, spectral_weight, spread, gather, tz, lx, ly, liy, lix)
    out = pl.pallas_call(
        final_kernel,
        grid=(x_local,),
        out_shape=jax.ShapeDtypeStruct(field.shape, F32),
        in_specs=[
            pl.BlockSpec((CT, G, 8, 128), lambda x: (0, 0, x, 0)),
            pl.BlockSpec((CH, 1, 16, NZ), lambda x: (0, x, 0, 0)),
            pl.BlockSpec((CH, CH), lambda x: (0, 0)),
            pl.BlockSpec((1, CH), lambda x: (0, 0)),
            pl.BlockSpec(ez.shape, lambda x: (0, 0)),
            pl.BlockSpec(el.shape, lambda x: (0, 0)),
        ],
        out_specs=pl.BlockSpec((CH, 1, 16, NZ), lambda x: (0, x, 0, 0)),
        scratch_shapes=[pltpu.VMEM((384, 384), BF), pltpu.VMEM((384, 384), BF), pltpu.VMEM((384, 128), F32)],
        compiler_params=pltpu.CompilerParams(vmem_limit_bytes=56 * 1024 * 1024),
        name="physical",
    )(modes, field, pointwise_weight, channel_bias.reshape(1, CH), ez, el)
    return out.reshape((1,) + out.shape)


def solution(mesh):
    in_specs = (P(None, None, "px", "py", None), P(None, "py", None, "px", None), P(), P())
    out_specs = P(None, None, "px", "py", None)
    return jax.shard_map(shards, mesh=mesh, in_specs=in_specs, out_specs=out_specs, check_vma=False)
```

time: 291 us -> 84.1 us (0.29)
  the two profiles are of different devices: /device:TPU:25 before, /device:TPU:1 now
where the time goes in v1:
time: 84.1 us; the launch traced here: 84 us
  Pallas kernels  84 us (100%)
    pallas_call x1, Pallas kernels, shards(): pl.pallas_call(spectral_kernel, out_shape=jax.ShapeDtypeStruct((CT, G, 64...  65.2 us
    pallas_call x1, Pallas kernels, shards(): pl.pallas_call(final_kernel, grid=(x_local,), out_shape=jax.ShapeDtypeStr...  18.8 us

profile of v1, /device:TPU:1, one launch (start us, length us, event | category | flops | bytes accessed | tf_op | source)
XLA Modules:
  0.0 84.0 jit_solution(15124205303320278556)
XLA Ops:
  0.0 65.2 %spectral.1.modes = f32[3,16,64,128]{3,2,1,0:T(8,128)} custom-call(f32[48,8,16,256]{3,2,1,0:T(8,128)} %bitcast.3, f32[2,4,32,2,2304]{4,3,2,1,0:T(2,128)} %weight.1, bf16[256,3072]{1,0:T(8,128)(2,1)} %constant.21.clone.spread, bf16[1536,384]{1,0:T(8,128)(2,1)} %constant.22.clone.gather, bf16[512,256]{1,0:T(8,128)(2,1)} %constant.18.clone.tz, ...), custom_call_target="tpu_custom_call" | custom-call | tf_op jit(solution)/shard_map/spectral/pallas_call | solution.py:378
  65.2 18.8 %physical.1 = f32[48,8,16,256]{3,2,1,0:T(8,128)} custom-call(f32[3,16,64,128]{3,2,1,0:T(8,128)} %spectral.1.modes, f32[48,8,16,256]{3,2,1,0:T(8,128)} %bitcast.4, f32[48,48]{1,0:T(8,128)} %point.1, f32[1,48]{1,0:T(1,128)} %bitcast.5, bf16[256,512]{1,0:T(8,128)(2,1)} %constant.25.clone.ez, bf16[128,512]{1,0:T(8,128)(2,1)} %constant.26.clone.el), custom_call_target="tpu_custom_call" | custom-call | tf_op jit(solution)/shard_map/physical/pallas_call | solution.py:388

commit v2 on v1

v2 whole, which is shorter than its diff:
```python
import functools
import math

import jax
import jax.numpy as jnp
import ml_dtypes
import numpy as np
from jax import lax
from jax.experimental import pallas as pl
from jax.experimental.pallas import tpu as pltpu
from jax.sharding import PartitionSpec as P

MESH = pl.DeviceIdType.MESH
BF = jnp.bfloat16
F32 = jnp.float32
ANY = pl.BlockSpec(memory_space=pl.ANY)
VMEM = pl.BlockSpec(memory_space=pltpu.VMEM)

NX, NY, NZ, MODES, CH, G, H = 128, 128, 256, 32, 48, 16, 8
CT = CH // 16
TA, TC, TB = range(3)


def halves(table):
    high = table.astype(ml_dtypes.bfloat16)
    low = (table - high.astype(np.float64)).astype(ml_dtypes.bfloat16)
    return high, low


def signed(modes):
    number = np.arange(modes)
    return np.where(number < modes // 2, number, number - modes)


def angles(position, mode, length):
    return 2.0 * math.pi * ((position[:, None] * mode[None, :]) % length) / length


def lane_parts():
    lane = np.arange(128)
    return lane // 64, (lane // 32) % 2, (lane // 16) % 2, lane % 16


@functools.cache
def constants():
    ri, y2, k2, low = lane_parts()
    k = 2 * low + k2
    a = angles(np.arange(NZ), k, NZ)
    wave = np.where(ri[None, :] == 0, np.cos(a), -np.sin(a))
    forward = np.concatenate([wave * (y2 == 0), wave * (y2 == 1)], axis=0)
    tz = np.concatenate(halves(forward), axis=1)
    gain = np.where(k == 0, 1.0, 2.0) / (NX * NY * NZ)
    eh, el = halves((forward * gain).T)
    ez = np.concatenate([eh, eh], axis=0)
    f = signed(MODES)
    ax = angles(np.arange(NX), f, NX)
    ch, cl = halves(np.concatenate([np.cos(ax).T, np.sin(ax).T], axis=0))
    lx = np.concatenate(
        [np.concatenate([ch, ch], axis=1), np.concatenate([cl, np.zeros_like(cl)], axis=1)], axis=0
    )
    ch, cl = halves(np.concatenate([np.cos(ax), np.sin(ax)], axis=0))
    lix = np.concatenate([ch, ch, cl], axis=1)
    y = np.arange(NY).reshape(H, 2, 8)
    parts = [y[:, h].reshape(-1) for h in range(2)]
    ay = [angles(p, f, NY) for p in parts]
    rows = np.concatenate([t for q in ay for t in (np.cos(q).T, np.sin(q).T)], axis=0)
    ch, cl = halves(rows)
    ly = np.concatenate(
        [np.concatenate([ch, ch], axis=1), np.concatenate([cl, np.zeros_like(cl)], axis=1)], axis=0
    )
    rows = np.concatenate([np.cos(ay[0]), np.cos(ay[1]), np.sin(ay[0]), np.sin(ay[1])], axis=0)
    ch, cl = halves(rows)
    liy = np.concatenate([ch, ch, cl], axis=1)
    pair = np.zeros((128, 4, 2, 8, CH))
    both = np.zeros((128, 2, 2, 2, 8, CH))
    for r in range(2):
        for c in range(32):
            pair[r * 64 + 32 + c, c // 8, r, c % 8, :] = 1.0
        for q in range(2):
            for c in range(16):
                both[r * 64 + 32 + q * 16 + c, c // 8, r, q, c % 8, :] = 1.0
    spread = np.stack([pair.reshape(128, -1), both.reshape(128, -1)])
    spread = np.concatenate([spread, spread], axis=1).astype(ml_dtypes.bfloat16)
    pair = np.zeros((2, 8, CH, 128))
    both = np.zeros((2, 2, 8, CH, 128))
    for r in range(2):
        for h in range(2):
            for o in range(32):
                pair[r, :, o, r * 64 + h * 32 + o] = 1.0
            for q in range(2):
                for o in range(16):
                    both[q, r, :, 32 + o, r * 64 + h * 32 + q * 16 + o] = 1.0
    gather = np.concatenate([pair.reshape(-1, 128), both.reshape(-1, 128)], axis=0).astype(ml_dtypes.bfloat16)
    return tz, lx, ly, spread, gather, liy, lix, ez, el


def split(value):
    high = value.astype(BF)
    return high, (value - high.astype(F32)).astype(BF)


def dot(a, b):
    return jnp.dot(a, b, preferred_element_type=F32)


def trade(a, b, step, lane):
    keep = (lane & step) == 0
    return jnp.where(keep, a, pltpu.roll(b, step, 1)), jnp.where(keep, pltpu.roll(a, 128 - step, 1), b)


def lanes16(tiles, lane):
    tiles = [pltpu.roll(tile, c, 1) if c else tile for c, tile in enumerate(tiles)]
    for bit in range(4):
        step = 1 << bit
        shift = (lane & step) != 0
        tiles = [jnp.where(shift, tiles[(h + step) % 16], tiles[h]) for h in range(16)]
    return [pltpu.roll(tiles[16 - g], 128 - g, 1) if g else tiles[0] for g in range(16)]


def gelu(v):
    return 0.5 * v * (1.0 + lax.erf(v * math.sqrt(0.5)))


def spectral_kernel(
    field, weight, spread, gather, ez, el, point, bias, tz, lx, ly, liy, lix, pre, last,
    f_in, w_in, e_in, r_in, ez_in, el_in, a_high, a_low, shift, held,
    send1, recv1, send2, recv2, send3, recv3, send4, recv4, v_exp, h_acc,
    f_sem, w_sem, c_sem, s1, r1, s2, r2, s3, r3, s4, r4, o_sem, p_sem,
):
    me, my = lax.axis_index("px"), lax.axis_index("py")

    def field_copy(t):
        return pltpu.make_async_copy(field.at[pl.ds(t * 16, 16)], f_in.at[pl.ds(t * 16, 16)], f_sem.at[t])

    def weight_copy(r, q):
        return pltpu.make_async_copy(weight.at[r, :, :, q, :], w_in.at[r, q], w_sem.at[r, q])

    const_copies = [
        pltpu.make_async_copy(spread, e_in, c_sem.at[0]),
        pltpu.make_async_copy(gather, r_in, c_sem.at[1]),
        pltpu.make_async_copy(ez, ez_in, c_sem.at[2]),
        pltpu.make_async_copy(el, el_in, c_sem.at[3]),
    ]
    for t in (2, 0, 1):
        field_copy(t).start()

    barrier = pltpu.get_barrier_semaphore()

    def greet_x(d, c):
        pl.semaphore_signal(barrier, inc=1, device_id=(lax.rem(me + d, G), my), device_id_type=MESH)
        return c

    def greet_y(d, c):
        pl.semaphore_signal(barrier, inc=1, device_id=(me, lax.rem(my + d, H)), device_id_type=MESH)
        return c

    lax.fori_loop(1, G, greet_x, 0)
    lax.fori_loop(1, H, greet_y, 0)

    def copy1(part, half, target, source):
        tiles, sem = (pl.ds(TB, 1), 1) if part else (pl.ds(TA, 2), 0)
        return pltpu.make_async_remote_copy(
            send1.at[tiles, target, pl.ds(half * 32, 32)], recv1.at[tiles, pl.ds(source * 64 + half * 32, 32)],
            s1.at[sem], r1.at[sem], device_id=(target, my), device_id_type=MESH)

    def send1_all(part, half):
        def body(d, c):
            copy1(part, half, lax.rem(me + d, G), me).start()
            return c
        lax.fori_loop(1, G, body, 0)

    def copy2(t, target, source):
        return pltpu.make_async_remote_copy(
            send2.at[t, pl.ds(target * 32, 32)], recv2.at[t, pl.ds(source * 32, 32)], s2.at[t],
            r2.at[t], device_id=(me, target), device_id_type=MESH)

    def copy3(t, target, source):
        return pltpu.make_async_remote_copy(
            send3.at[t, target], recv3.at[t, pl.ds(source * 32, 32)], s3.at[t], r3.at[t],
            device_id=(me, target), device_id_type=MESH)

    def copy4(t, target, source):
        return pltpu.make_async_remote_copy(
            send4.at[t, pl.ds(target * 64, 64)], recv4.at[t, source], s4.at[t], r4.at[t],
            device_id=(target, my), device_id_type=MESH)

    def send_all(copy, t, index, count):
        def body(d, c):
            copy(t, lax.rem(index + d, count), index).start()
            return c
        lax.fori_loop(1, count, body, 0)

    def all1(part):
        tiles = pl.ds(TB, 1) if part else pl.ds(TA, 2)
        return pltpu.make_async_remote_copy(
            send1.at[tiles, pl.ds(0, G - 1)], recv1.at[tiles, pl.ds(0, (G - 1) * 64)], s1.at[part], r1.at[part],
            device_id=(lax.rem(me + 1, G), my), device_id_type=MESH)

    def all2(t):
        return pltpu.make_async_remote_copy(
            send2.at[t, pl.ds(0, (H - 1) * 32)], recv2.at[t, pl.ds(0, (H - 1) * 32)], s2.at[t], r2.at[t],
            device_id=(me, lax.rem(my + 1, H)), device_id_type=MESH)

    def all3(t):
        return pltpu.make_async_remote_copy(
            send3.at[t, pl.ds(0, H - 1)], recv3.at[t, pl.ds(0, (H - 1) * 32)], s3.at[t], r3.at[t],
            device_id=(me, lax.rem(my + 1, H)), device_id_type=MESH)

    def all4(t):
        return pltpu.make_async_remote_copy(
            send4.at[t, pl.ds(0, (G - 1) * 64)], recv4.at[t, pl.ds(0, G - 1)], s4.at[t], r4.at[t],
            device_id=(lax.rem(me + 1, G), my), device_id_type=MESH)

    lane = lax.broadcasted_iota(jnp.int32, (8, 128), 1)
    wide = lax.broadcasted_iota(jnp.int32, (1, 128), 1)
    sign = jnp.where(wide < 64, 1.0, -1.0).astype(F32)
    first = (wide & 32) == 0

    def z_tiles(first_c, count, x, xs):
        block = f_in[first_c:first_c + count, pl.ds(x, xs)]
        rows = jnp.concatenate(
            [block[:, :, :8].reshape(count * xs * 8, NZ), block[:, :, 8:].reshape(count * xs * 8, NZ)], axis=1)
        high, low = split(rows)
        prod = dot(high, tz[...])
        z = (prod[:, :128] + prod[:, 128:] + dot(low, tz[:, :128])).reshape(count, xs, 8, 128)
        return [[lanes16([z[g * 16 + c, q] for c in range(16)], lane) for g in range(count // 16)] for q in range(xs)]

    def z_both(xq, c):
        for q, (tiles,) in enumerate(z_tiles(32, 16, xq * 4, 4)):
            for g in range(G):
                send1[TB, g, pl.ds(xq * 32 + q * 8, 8), :] = tiles[g]
        return c

    def z_pair(xq, c):
        for q, (even, odd) in enumerate(z_tiles(0, 32, xq * 2, 2)):
            for g in range(G):
                a, b = trade(even[g], odd[g], 16, lane)
                send1[TA, g, pl.ds(xq * 16 + q * 8, 8), :] = a
                send1[TC, g, pl.ds(xq * 16 + q * 8, 8), :] = b
        return c

    field_copy(2).wait()
    z_both(0, 0)
    pl.semaphore_wait(barrier, G + H - 2)
    send1_all(1, 0)
    z_both(1, 0)
    send1_all(1, 1)
    field_copy(0).wait()
    field_copy(1).wait()
    for half in range(2):
        lax.fori_loop(half * 2, half * 2 + 2, z_pair, 0)
        send1_all(0, half)
    for t in range(CT):
        recv1[t, pl.ds(me * 64, 64), :] = send1[t, me]

    for copy in const_copies:
        copy.start()
    for r in range(2):
        for q in range(2):
            weight_copy(r, q).start()

    row = lax.broadcasted_iota(jnp.int32, (384, CH), 0)
    col = lax.broadcasted_iota(jnp.int32, (384, CH), 1)
    pick = row // 8 == col
    shift[...] = jnp.sum(jnp.where(pick, bias[...], 0.0), axis=1, keepdims=True) + jnp.zeros((384, 128), F32)
    picked = pick.astype(F32).astype(BF)
    row = lax.broadcasted_iota(jnp.int32, (384, 384), 0)
    col = lax.broadcasted_iota(jnp.int32, (384, 384), 1)
    same = (row % 8) == (col % 8)
    for piece, ref in zip(split(point[...]), (a_high, a_low)):
        tall = lax.dot_general(picked, piece, (((1,), (1,)), ((), ())), preferred_element_type=F32)
        full = lax.dot_general(tall.astype(BF), picked, (((1,), (1,)), ((), ())), preferred_element_type=F32)
        ref[...] = jnp.where(same, full, 0.0).astype(BF)

    def local_step(x, c):
        for h in range(2):
            high, low = split(f_in[:, x, h * 8:(h + 1) * 8, :].reshape(384, NZ))
            local = dot(a_high[...], high) + dot(a_low[...], high) + dot(a_high[...], low) + shift[:, :1]
            held[:, x, h * 8:(h + 1) * 8, :] = local.reshape(CH, 8, NZ)
        return c

    lax.fori_loop(0, 8, local_step, 0)

    def pre_copy(t):
        return pltpu.make_async_copy(held.at[pl.ds(t * 16, 16)], pre.at[pl.ds(t * 16, 16)], p_sem.at[t])

    def along_x(t):
        for pair in range(4):
            data = jnp.concatenate(
                [recv1[t, pl.ds(2 * pair + h, 128, stride=8), :] for h in range(2)], axis=1)
            prod = dot(lx[...], jnp.concatenate(split(data), axis=0))
            prod = prod[:64] + prod[64:]
            for h in range(2):
                piece = prod[:, h * 128:(h + 1) * 128]
                send2[t, pl.ds(2 * pair + h, 32, stride=8), :] = piece[:32] + sign * pltpu.roll(piece[32:], 64, 1)
        send_all(copy2, t, my, H)
        recv2[t, pl.ds(my * 32, 32), :] = send2[t, pl.ds(my * 32, 32), :]

    def along_y(t):
        all2(t).wait_recv()
        data = recv2[t].reshape(H, 4, 8, 128)
        data = jnp.concatenate([data[:, i].reshape(64, 128) for i in range(4)], axis=1)
        prod = dot(ly[...], jnp.concatenate(split(data), axis=0))
        prod = prod[:128] + prod[128:]
        rows = []
        for i in range(4):
            piece = prod[:, i * 128:(i + 1) * 128]
            u = jnp.where(first, piece[:32], piece[64:96])
            w = jnp.where(first, piece[32:64], piece[96:])
            v = u + sign * pltpu.roll(w, 64, 1)
            rows.append(v + pltpu.roll(v, 32, 1))
        v = jnp.concatenate(rows, axis=0)
        v_exp[t] = dot(jnp.concatenate(split(v), axis=1), e_in[1 if t == TB else 0])

    def mix(q):
        t = (TA, TC)[q]

        def body(i, c):
            at = pl.ds(pl.multiple_of(i * 32, 32), 32)
            for part in range(3):
                real = jnp.zeros((32, 128), F32)
                imag = jnp.zeros((32, 128), F32)
                for b in range(6):
                    col = b * 384 + part * 128
                    if b < 4:
                        source, base, gap = t, b * 768 + part * 128, 384
                    else:
                        source, base, gap = TB, (b - 4) * 1536 + q * 384 + part * 128, 768
                    vr = v_exp[source, at, base:base + 128]
                    vi = v_exp[source, at, base + gap:base + gap + 128]
                    w0 = w_in[0, q, i, :, col:col + 128]
                    w1 = w_in[1, q, i, :, col:col + 128]
                    real += vr * w0 - vi * w1
                    imag += vr * w1 + vi * w0
                col = q * 768 + part * 128
                h_acc[at, col:col + 128] = real
                h_acc[at, col + 384:col + 384 + 128] = imag
            return c

        lax.fori_loop(0, 4, body, 0)

    def collect(t):
        if t == TB:
            source, table = h_acc[...], r_in[768:, :]
        else:
            source, table = h_acc[:, (0 if t == TA else 768):(768 if t == TA else 1536)], r_in[:768, :]
        high, low = split(source)
        return dot(high, table) + dot(low, table)

    def back_y(t):
        h_all = collect(t)
        data = jnp.concatenate([h_all[i * 32:(i + 1) * 32] for i in range(4)], axis=1)
        high, low = split(data)
        prod = dot(liy[...], jnp.concatenate([high, low, high], axis=0))
        for i in range(4):
            piece = prod[:, i * 128:(i + 1) * 128]
            a = jnp.where(first, piece[:64], piece[64:128])
            b = jnp.where(first, piece[128:192], piece[192:])
            q = a - sign * pltpu.roll(b, 64, 1)
            send3[t, :, i * 8:(i + 1) * 8, :] = q.reshape(H, 8, 128)
        send_all(copy3, t, my, H)
        recv3[t, pl.ds(my * 32, 32), :] = send3[t, my]

    def back_x(t):
        all3(t).wait_recv()
        for pair in range(4):
            data = jnp.concatenate(
                [recv3[t, pl.ds(2 * pair + h, 32, stride=8), :] for h in range(2)], axis=1)
            high, low = split(data)
            prod = dot(lix[...], jnp.concatenate([high, low, high], axis=0))
            for h in range(2):
                piece = prod[:, h * 128:(h + 1) * 128]
                send4[t, pl.ds(2 * pair + h, 128, stride=8), :] = piece[:128] - sign * pltpu.roll(piece[128:], 64, 1)
        send_all(copy4, t, me, G)
        recv4[t, me] = send4[t, pl.ds(me * 64, 64), :]

    pre_copy(CT - 1).start()
    all1(1).wait_recv()
    along_x(TB)
    all1(0).wait_recv()
    along_x(TA)
    along_x(TC)
    for copy in const_copies:
        copy.wait()
    for r in range(2):
        for q in range(2):
            weight_copy(r, q).wait()
    along_y(TB)
    along_y(TA)
    mix(0)
    back_y(TA)
    along_y(TC)
    mix(1)
    back_y(TC)
    back_y(TB)
    back_x(TA)
    back_x(TC)
    back_x(TB)

    all1(0).wait_send()
    all1(1).wait_send()
    for t in range(CT):
        all2(t).wait_send()
        all3(t).wait_send()
    all4(TA).wait_recv()
    all4(TC).wait_recv()

    def finish(xq, c):
        tiles = []
        for x in range(2):
            at = pl.ds(xq * 16 + x * 8, 8)
            even = lanes16([recv4[TA, s, at, :] for s in range(G)], lane)
            odd = lanes16([recv4[TC, s, at, :] for s in range(G)], lane)
            tiles.append([trade(a, b, 16, lane) for a, b in zip(even, odd)])
        rows = jnp.concatenate([tiles[x][o][p] for p in range(2) for o in range(16) for x in range(2)], axis=0)
        high, low = split(rows)
        spectral = dot(jnp.concatenate([high, low], axis=1), ez_in[...]) + dot(high, el_in[...])
        for h in range(2):
            at = (pl.ds(0, 32), pl.ds(xq * 2, 2), pl.ds(h * 8, 8), slice(None))
            held[at] = gelu(held[at] + spectral[:, h * NZ:(h + 1) * NZ].reshape(32, 2, 8, NZ))
        return c

    lax.fori_loop(0, 4, finish, 0)
    for t in range(CT - 1):
        pre_copy(t).start()
    for t in range(CT):
        all4(t).wait_send()
    all4(TB).wait_recv()
    copy = pltpu.make_async_copy(recv4.at[TB], last, o_sem)
    copy.start()
    copy.wait()
    for t in range(CT):
        pre_copy(t).wait()


def final_kernel(pre, modes, ez, el, out, through, work, m_in, ez_in, el_in, t_sem, w_sem, o_sem, v_sem, c_sem):
    lane = lax.broadcasted_iota(jnp.int32, (8, 128), 1)
    done = CH - 16
    small = [
        pltpu.make_async_copy(modes, m_in, c_sem.at[0]),
        pltpu.make_async_copy(ez, ez_in, c_sem.at[1]),
        pltpu.make_async_copy(el, el_in, c_sem.at[2]),
    ]
    load = [pltpu.make_async_copy(pre.at[pl.ds(done, 16), pl.ds(2 * p, 2)], work.at[p], w_sem.at[p]) for p in range(4)]
    store = [pltpu.make_async_copy(work.at[p], out.at[pl.ds(done, 16), pl.ds(2 * p, 2)], v_sem.at[p]) for p in range(4)]
    take = [pltpu.make_async_copy(pre.at[pl.ds(8 * p, 8)], through.at[p], t_sem.at[p]) for p in range(4)]
    give = [pltpu.make_async_copy(through.at[p], out.at[pl.ds(8 * p, 8)], o_sem.at[p]) for p in range(4)]
    for copy in small + load[:1] + take[:1] + load[1:] + take[1:]:
        copy.start()
    for copy in small:
        copy.wait()
    for p in range(4):
        load[p].wait()
        tiles = [lanes16([m_in[s, p * 16 + x * 8:p * 16 + (x + 1) * 8, :] for s in range(G)], lane) for x in range(2)]
        high, low = split(jnp.concatenate([tile[o] for o in range(16) for tile in tiles], axis=0))
        spectral = dot(jnp.concatenate([high, low], axis=1), ez_in[...]) + dot(high, el_in[...])
        for h in range(2):
            at = (p, slice(None), slice(None), slice(h * 8, (h + 1) * 8), slice(None))
            work[at] = gelu(work[at] + spectral[:, h * NZ:(h + 1) * NZ].reshape(16, 2, 8, NZ))
        store[p].start()
        take[p].wait()
        give[p].start()
    for copy in store + give:
        copy.wait()


def shards(field, spectral_weight, pointwise_weight, channel_bias):
    tz, lx, ly, spread, gather, liy, lix, ez, el = [jnp.asarray(c) for c in constants()]
    field = field.reshape(field.shape[1:])
    scratch = [
        pltpu.VMEM((CH, 8, 16, NZ), F32),
        pltpu.VMEM((2, 2, 4, MODES, CH * CH), F32),
        pltpu.VMEM(spread.shape, BF),
        pltpu.VMEM(gather.shape, BF),
        pltpu.VMEM(ez.shape, BF),
        pltpu.VMEM(el.shape, BF),
        pltpu.VMEM((384, 384), BF),
        pltpu.VMEM((384, 384), BF),
        pltpu.VMEM((384, 128), F32),
        pltpu.VMEM((CH, 8, 16, NZ), F32),
        pltpu.VMEM((CT, G, 64, 128), F32),
        pltpu.VMEM((CT, G * 64, 128), F32),
        pltpu.VMEM((CT, H * 32, 128), F32),
        pltpu.VMEM((CT, H * 32, 128), F32),
        pltpu.VMEM((CT, H, 32, 128), F32),
        pltpu.VMEM((CT, H * 32, 128), F32),
        pltpu.VMEM((CT, G * 64, 128), F32),
        pltpu.VMEM((CT, G, 64, 128), F32),
        pltpu.VMEM((CT, 128, 3072), F32),
        pltpu.VMEM((128, 1536), F32),
    ]
    dma = pltpu.SemaphoreType.DMA
    scratch += [dma((CT,)), dma((2, 2)), dma((4,))]
    scratch += [dma((CT,))] * 8 + [dma, dma((CT,))]
    pre, last = pl.pallas_call(
        spectral_kernel,
        out_shape=[jax.ShapeDtypeStruct(field.shape, F32), jax.ShapeDtypeStruct((G, 64, 128), F32)],
        in_specs=[ANY] * 6 + [VMEM] * 7,
        out_specs=[ANY] * 2,
        scratch_shapes=scratch,
        compiler_params=pltpu.CompilerParams(
            collective_id=0, has_side_effects=True, vmem_limit_bytes=60 * 1024 * 1024),
        name="spectral",
    )(field, spectral_weight, spread, gather, ez, el, pointwise_weight, channel_bias.reshape(1, CH),
      tz, lx, ly, liy, lix)
    out = pl.pallas_call(
        final_kernel,
        out_shape=jax.ShapeDtypeStruct(field.shape, F32),
        in_specs=[ANY] * 4,
        out_specs=ANY,
        scratch_shapes=[
            pltpu.VMEM((4, 8, 8, 16, NZ), F32),
            pltpu.VMEM((4, 16, 2, 16, NZ), F32),
            pltpu.VMEM((G, 64, 128), F32),
            pltpu.VMEM(ez.shape, BF),
            pltpu.VMEM(el.shape, BF),
            dma((4,)), dma((4,)), dma((4,)), dma((4,)), dma((3,)),
        ],
        compiler_params=pltpu.CompilerParams(vmem_limit_bytes=60 * 1024 * 1024),
        name="physical",
    )(pre, last, ez, el)
    return out.reshape((1,) + out.shape)


def solution(mesh):
    in_specs = (P(None, None, "px", "py", None), P(None, "py", None, "px", None), P(), P())
    out_specs = P(None, None, "px", "py", None)
    return jax.shard_map(shards, mesh=mesh, in_specs=in_specs, out_specs=out_specs, check_vma=False)
```

time: 84.1 us -> 68.5 us (0.81)
  Pallas kernels: 84 us -> 68.1 us
    pallas_call x2, Pallas kernels: 84 us -> 68.1 us  [the longest x1 62.2 us: shards(): pl.pallas_call(spectral_kernel, out_shape=[jax.ShapeDtypeStruct(field.sha...]
where the time goes in v2:
time: 68.5 us; the launch traced here: 68.1 us
  Pallas kernels  68.1 us (99%)
    pallas_call x1, Pallas kernels, shards(): pl.pallas_call(spectral_kernel, out_shape=[jax.ShapeDtypeStruct(field.sha...  62.2 us
    pallas_call x1, Pallas kernels, shards(): pl.pallas_call(final_kernel, out_shape=jax.ShapeDtypeStruct(field.shape,...  5.87 us

profile of v2, /device:TPU:1, one launch (start us, length us, event | category | flops | bytes accessed | tf_op | source)
XLA Modules:
  0.0 68.1 jit_solution(7508506424354348032)
XLA Ops:
  0.0 62.2 %spectral.1 = (f32[48,8,16,256]{3,2,1,0:T(8,128)}, f32[16,64,128]{2,1,0:T(8,128)}) custom-call(f32[48,8,16,256]{3,2,1,0:T(8,128)} %bitcast.3, f32[2,4,32,2,2304]{4,3,2,1,0:T(2,128)} %weight.1, bf16[2,256,3072]{2,1,0:T(8,128)(2,1)} %constant.21.clone.spread, bf16[2304,128]{1,0:T(8,128)(2,1)} %constant.22.clone.gather, bf16[256,512]{1,0:T(8,128)(2,1)} %constant.25.clone.ez, ...), custom_call_target="tpu_custom_call" | custom-call | tf_op jit(solution)/shard_map/spectral/pallas_call | solution.py:495
  62.2 5.9 %physical.1 = f32[48,8,16,256]{3,2,1,0:T(8,128)} custom-call(f32[48,8,16,256]{3,2,1,0:T(8,128)} %get-tuple-element.7.pre, f32[16,64,128]{2,1,0:T(8,128)} %get-tuple-element.8.modes, bf16[256,512]{1,0:T(8,128)(2,1)} %constant.25.clone.ez, bf16[128,512]{1,0:T(8,128)(2,1)} %constant.26.clone.el), custom_call_target="tpu_custom_call" | custom-call | tf_op jit(solution)/shard_map/physical/pallas_call | solution.py:506

commit v3 on v2

--- a/solution.py
+++ b/solution.py
@@ -122,10 +122,10 @@
 
 
 def spectral_kernel(
-    field, weight, spread, gather, ez, el, point, bias, tz, lx, ly, liy, lix, pre, last,
-    f_in, w_in, e_in, r_in, ez_in, el_in, a_high, a_low, shift, held,
+    field, weight, spread, gather, ez, el, point_far, bias_far, tz_far, lx_far, ly_far, liy_far, lix_far, held, last,
+    f_in, w_in, e_in, r_in, ez_in, el_in, tz, lx, ly, liy, lix, point, bias, a_high, a_low, shift,
     send1, recv1, send2, recv2, send3, recv3, send4, recv4, v_exp, h_acc,
-    f_sem, w_sem, c_sem, s1, r1, s2, r2, s3, r3, s4, r4, o_sem, p_sem,
+    f_sem, w_sem, c_sem, s1, r1, s2, r2, s3, r3, s4, r4, o_sem,
 ):
     me, my = lax.axis_index("px"), lax.axis_index("py")
 
@@ -140,7 +140,17 @@
         pltpu.make_async_copy(gather, r_in, c_sem.at[1]),
         pltpu.make_async_copy(ez, ez_in, c_sem.at[2]),
         pltpu.make_async_copy(el, el_in, c_sem.at[3]),
+        pltpu.make_async_copy(lx_far, lx, c_sem.at[4]),
+        pltpu.make_async_copy(ly_far, ly, c_sem.at[5]),
+        pltpu.make_async_copy(liy_far, liy, c_sem.at[6]),
+        pltpu.make_async_copy(lix_far, lix, c_sem.at[7]),
     ]
+    conv_copies = [
+        pltpu.make_async_copy(point_far, point, c_sem.at[9]),
+        pltpu.make_async_copy(bias_far, bias, c_sem.at[10]),
+    ]
+    first_table = pltpu.make_async_copy(tz_far, tz, c_sem.at[8])
+    first_table.start()
     for t in (2, 0, 1):
         field_copy(t).start()
 
@@ -157,15 +167,14 @@
     lax.fori_loop(1, G, greet_x, 0)
     lax.fori_loop(1, H, greet_y, 0)
 
-    def copy1(part, half, target, source):
-        tiles, sem = (pl.ds(TB, 1), 1) if part else (pl.ds(TA, 2), 0)
-        return pltpu.make_async_remote_copy(
-            send1.at[tiles, target, pl.ds(half * 32, 32)], recv1.at[tiles, pl.ds(source * 64 + half * 32, 32)],
-            s1.at[sem], r1.at[sem], device_id=(target, my), device_id_type=MESH)
-
-    def send1_all(part, half):
+    def copy1(t, first_row, rows, target, source):
+        return pltpu.make_async_remote_copy(
+            send1.at[t, target, pl.ds(first_row, rows)], recv1.at[t, pl.ds(source * 64 + first_row, rows)],
+            s1.at[t], r1.at[t], device_id=(target, my), device_id_type=MESH)
+
+    def send1_all(t, first_row, rows):
         def body(d, c):
-            copy1(part, half, lax.rem(me + d, G), me).start()
+            copy1(t, first_row, rows, lax.rem(me + d, G), me).start()
             return c
         lax.fori_loop(1, G, body, 0)
 
@@ -179,10 +188,16 @@
             send3.at[t, target], recv3.at[t, pl.ds(source * 32, 32)], s3.at[t], r3.at[t],
             device_id=(me, target), device_id_type=MESH)
 
+    def landing(t):
+        return last if t == TB else recv4.at[t]
+
     def copy4(t, target, source):
         return pltpu.make_async_remote_copy(
-            send4.at[t, pl.ds(target * 64, 64)], recv4.at[t, source], s4.at[t], r4.at[t],
+            send4.at[t, pl.ds(target * 64, 64)], landing(t).at[source], s4.at[t], r4.at[t],
             device_id=(target, my), device_id_type=MESH)
+
+    def own4():
+        return pltpu.make_async_copy(send4.at[TB, pl.ds(me * 64, 64)], last.at[me], o_sem)
 
     def send_all(copy, t, index, count):
         def body(d, c):
@@ -190,10 +205,9 @@
             return c
         lax.fori_loop(1, count, body, 0)
 
-    def all1(part):
-        tiles = pl.ds(TB, 1) if part else pl.ds(TA, 2)
-        return pltpu.make_async_remote_copy(
-            send1.at[tiles, pl.ds(0, G - 1)], recv1.at[tiles, pl.ds(0, (G - 1) * 64)], s1.at[part], r1.at[part],
+    def all1(t):
+        return pltpu.make_async_remote_copy(
+            send1.at[t, pl.ds(0, G - 1)], recv1.at[t, pl.ds(0, (G - 1) * 64)], s1.at[t], r1.at[t],
             device_id=(lax.rem(me + 1, G), my), device_id_type=MESH)
 
     def all2(t):
@@ -208,7 +222,7 @@
 
     def all4(t):
         return pltpu.make_async_remote_copy(
-            send4.at[t, pl.ds(0, (G - 1) * 64)], recv4.at[t, pl.ds(0, G - 1)], s4.at[t], r4.at[t],
+            send4.at[t, pl.ds(0, (G - 1) * 64)], landing(t).at[pl.ds(0, G - 1)], s4.at[t], r4.at[t],
             device_id=(lax.rem(me + 1, G), my), device_id_type=MESH)
 
     lane = lax.broadcasted_iota(jnp.int32, (8, 128), 1)
@@ -239,17 +253,21 @@
                 send1[TC, g, pl.ds(xq * 16 + q * 8, 8), :] = b
         return c
 
+    first_table.wait()
     field_copy(2).wait()
     z_both(0, 0)
     pl.semaphore_wait(barrier, G + H - 2)
-    send1_all(1, 0)
+    send1_all(TB, 0, 32)
+    for copy in conv_copies:
+        copy.start()
     z_both(1, 0)
-    send1_all(1, 1)
+    send1_all(TB, 32, 32)
     field_copy(0).wait()
     field_copy(1).wait()
     for half in range(2):
         lax.fori_loop(half * 2, half * 2 + 2, z_pair, 0)
-        send1_all(0, half)
+        send1_all(TA, half * 32, 32)
+    send1_all(TC, 0, 64)
     for t in range(CT):
         recv1[t, pl.ds(me * 64, 64), :] = send1[t, me]
 
@@ -259,6 +277,8 @@
         for q in range(2):
             weight_copy(r, q).start()
 
+    for copy in conv_copies:
+        copy.wait()
     row = lax.broadcasted_iota(jnp.int32, (384, CH), 0)
     col = lax.broadcasted_iota(jnp.int32, (384, CH), 1)
     pick = row // 8 == col
@@ -280,9 +300,6 @@
         return c
 
     lax.fori_loop(0, 8, local_step, 0)
-
-    def pre_copy(t):
-        return pltpu.make_async_copy(held.at[pl.ds(t * 16, 16)], pre.at[pl.ds(t * 16, 16)], p_sem.at[t])
 
     def along_x(t):
         for pair in range(4):
@@ -372,46 +389,55 @@
                 piece = prod[:, h * 128:(h + 1) * 128]
                 send4[t, pl.ds(2 * pair + h, 128, stride=8), :] = piece[:128] - sign * pltpu.roll(piece[128:], 64, 1)
         send_all(copy4, t, me, G)
-        recv4[t, me] = send4[t, pl.ds(me * 64, 64), :]
-
-    pre_copy(CT - 1).start()
-    all1(1).wait_recv()
-    along_x(TB)
-    all1(0).wait_recv()
-    along_x(TA)
-    along_x(TC)
+        if t == TB:
+            own4().start()
+        else:
+            recv4[t, me] = send4[t, pl.ds(me * 64, 64), :]
+
     for copy in const_copies:
         copy.wait()
+    all1(TB).wait_recv()
+    along_x(TB)
+    all1(TA).wait_recv()
+    along_x(TA)
     for r in range(2):
         for q in range(2):
             weight_copy(r, q).wait()
     along_y(TB)
+    all1(TC).wait_recv()
+    along_x(TC)
     along_y(TA)
     mix(0)
     back_y(TA)
     along_y(TC)
     mix(1)
     back_y(TC)
+    back_x(TA)
     back_y(TB)
-    back_x(TA)
     back_x(TC)
     back_x(TB)
 
-    all1(0).wait_send()
-    all1(1).wait_send()
     for t in range(CT):
+        all1(t).wait_send()
         all2(t).wait_send()
         all3(t).wait_send()
     all4(TA).wait_recv()
+
+    def turn(x, c):
+        at = pl.ds(pl.multiple_of(x * 8, 8), 8)
+        for o, tile in enumerate(lanes16([recv4[TA, s, at, :] for s in range(G)], lane)):
+            recv4[TA, o, at, :] = tile
+        return c
+
+    lax.fori_loop(0, 8, turn, 0)
     all4(TC).wait_recv()
 
     def finish(xq, c):
         tiles = []
         for x in range(2):
             at = pl.ds(xq * 16 + x * 8, 8)
-            even = lanes16([recv4[TA, s, at, :] for s in range(G)], lane)
             odd = lanes16([recv4[TC, s, at, :] for s in range(G)], lane)
-            tiles.append([trade(a, b, 16, lane) for a, b in zip(even, odd)])
+            tiles.append([trade(recv4[TA, o, at, :], odd[o], 16, lane) for o in range(16)])
         rows = jnp.concatenate([tiles[x][o][p] for p in range(2) for o in range(16) for x in range(2)], axis=0)
         high, low = split(rows)
         spectral = dot(jnp.concatenate([high, low], axis=1), ez_in[...]) + dot(high, el_in[...])
@@ -421,51 +447,41 @@
         return c
 
     lax.fori_loop(0, 4, finish, 0)
-    for t in range(CT - 1):
-        pre_copy(t).start()
     for t in range(CT):
         all4(t).wait_send()
+    own4().wait()
     all4(TB).wait_recv()
-    copy = pltpu.make_async_copy(recv4.at[TB], last, o_sem)
-    copy.start()
-    copy.wait()
-    for t in range(CT):
-        pre_copy(t).wait()
-
-
-def final_kernel(pre, modes, ez, el, out, through, work, m_in, ez_in, el_in, t_sem, w_sem, o_sem, v_sem, c_sem):
+
+
+def final_kernel(pre, modes, ez, el, out, work, ez_in, el_in, v_sem, o_sem, c_sem):
     lane = lax.broadcasted_iota(jnp.int32, (8, 128), 1)
     done = CH - 16
-    small = [
-        pltpu.make_async_copy(modes, m_in, c_sem.at[0]),
-        pltpu.make_async_copy(ez, ez_in, c_sem.at[1]),
-        pltpu.make_async_copy(el, el_in, c_sem.at[2]),
-    ]
-    load = [pltpu.make_async_copy(pre.at[pl.ds(done, 16), pl.ds(2 * p, 2)], work.at[p], w_sem.at[p]) for p in range(4)]
+    small = [pltpu.make_async_copy(ez, ez_in, c_sem.at[0]), pltpu.make_async_copy(el, el_in, c_sem.at[1])]
     store = [pltpu.make_async_copy(work.at[p], out.at[pl.ds(done, 16), pl.ds(2 * p, 2)], v_sem.at[p]) for p in range(4)]
-    take = [pltpu.make_async_copy(pre.at[pl.ds(8 * p, 8)], through.at[p], t_sem.at[p]) for p in range(4)]
-    give = [pltpu.make_async_copy(through.at[p], out.at[pl.ds(8 * p, 8)], o_sem.at[p]) for p in range(4)]
-    for copy in small + load[:1] + take[:1] + load[1:] + take[1:]:
+    give = [pltpu.make_async_copy(pre.at[pl.ds(8 * p, 8)], out.at[pl.ds(8 * p, 8)], o_sem.at[p]) for p in range(4)]
+    for copy in small + give:
         copy.start()
     for copy in small:
         copy.wait()
     for p in range(4):
-        load[p].wait()
-        tiles = [lanes16([m_in[s, p * 16 + x * 8:p * 16 + (x + 1) * 8, :] for s in range(G)], lane) for x in range(2)]
+        tiles = [lanes16([modes[s, p * 16 + x * 8:p * 16 + (x + 1) * 8, :] for s in range(G)], lane) for x in range(2)]
         high, low = split(jnp.concatenate([tile[o] for o in range(16) for tile in tiles], axis=0))
         spectral = dot(jnp.concatenate([high, low], axis=1), ez_in[...]) + dot(high, el_in[...])
         for h in range(2):
-            at = (p, slice(None), slice(None), slice(h * 8, (h + 1) * 8), slice(None))
-            work[at] = gelu(work[at] + spectral[:, h * NZ:(h + 1) * NZ].reshape(16, 2, 8, NZ))
+            y = slice(h * 8, (h + 1) * 8)
+            part = spectral[:, h * NZ:(h + 1) * NZ].reshape(16, 2, 8, NZ)
+            work[p, :, :, y, :] = gelu(pre[done:, 2 * p:2 * p + 2, y, :] + part)
         store[p].start()
-        take[p].wait()
-        give[p].start()
     for copy in store + give:
         copy.wait()
 
 
+def far(array):
+    return pltpu.with_memory_space_constraint(array, pltpu.HBM)
+
+
 def shards(field, spectral_weight, pointwise_weight, channel_bias):
-    tz, lx, ly, spread, gather, liy, lix, ez, el = [jnp.asarray(c) for c in constants()]
+    tz, lx, ly, spread, gather, liy, lix, ez, el = [far(jnp.asarray(c)) for c in constants()]
     field = field.reshape(field.shape[1:])
     scratch = [
         pltpu.VMEM((CH, 8, 16, NZ), F32),
@@ -474,10 +490,16 @@
         pltpu.VMEM(gather.shape, BF),
         pltpu.VMEM(ez.shape, BF),
         pltpu.VMEM(el.shape, BF),
+        pltpu.VMEM(tz.shape, BF),
+        pltpu.VMEM(lx.shape, BF),
+        pltpu.VMEM(ly.shape, BF),
+        pltpu.VMEM(liy.shape, BF),
+        pltpu.VMEM(lix.shape, BF),
+        pltpu.VMEM((CH, CH), F32),
+        pltpu.VMEM((1, CH), F32),
         pltpu.VMEM((384, 384), BF),
         pltpu.VMEM((384, 384), BF),
         pltpu.VMEM((384, 128), F32),
-        pltpu.VMEM((CH, 8, 16, NZ), F32),
         pltpu.VMEM((CT, G, 64, 128), F32),
         pltpu.VMEM((CT, G * 64, 128), F32),
         pltpu.VMEM((CT, H * 32, 128), F32),
@@ -485,38 +507,36 @@
         pltpu.VMEM((CT, H, 32, 128), F32),
         pltpu.VMEM((CT, H * 32, 128), F32),
         pltpu.VMEM((CT, G * 64, 128), F32),
-        pltpu.VMEM((CT, G, 64, 128), F32),
+        pltpu.VMEM((2, G, 64, 128), F32),
         pltpu.VMEM((CT, 128, 3072), F32),
         pltpu.VMEM((128, 1536), F32),
     ]
     dma = pltpu.SemaphoreType.DMA
-    scratch += [dma((CT,)), dma((2, 2)), dma((4,))]
-    scratch += [dma((CT,))] * 8 + [dma, dma((CT,))]
+    scratch += [dma((CT,)), dma((2, 2)), dma((11,))]
+    scratch += [dma((CT,))] * 8 + [dma]
     pre, last = pl.pallas_call(
         spectral_kernel,
-        out_shape=[jax.ShapeDtypeStruct(field.shape, F32), jax.ShapeDtypeStruct((G, 64, 128), F32)],
-        in_specs=[ANY] * 6 + [VMEM] * 7,
-        out_specs=[ANY] * 2,
+        out_shape=[pltpu.VMEM(field.shape, F32), pltpu.VMEM((G, 64, 128), F32)],
+        in_specs=[ANY] * 13,
+        out_specs=[VMEM] * 2,
         scratch_shapes=scratch,
         compiler_params=pltpu.CompilerParams(
-            collective_id=0, has_side_effects=True, vmem_limit_bytes=60 * 1024 * 1024),
+            collective_id=0, has_side_effects=True, vmem_limit_bytes=46 * 1024 * 1024),
         name="spectral",
-    )(field, spectral_weight, spread, gather, ez, el, pointwise_weight, channel_bias.reshape(1, CH),
+    )(far(field), far(spectral_weight), spread, gather, ez, el, far(pointwise_weight), far(channel_bias.reshape(1, CH)),
       tz, lx, ly, liy, lix)
     out = pl.pallas_call(
         final_kernel,
         out_shape=jax.ShapeDtypeStruct(field.shape, F32),
-        in_specs=[ANY] * 4,
+        in_specs=[VMEM, VMEM, ANY, ANY],
         out_specs=ANY,
         scratch_shapes=[
-            pltpu.VMEM((4, 8, 8, 16, NZ), F32),
             pltpu.VMEM((4, 16, 2, 16, NZ), F32),
-            pltpu.VMEM((G, 64, 128), F32),
             pltpu.VMEM(ez.shape, BF),
             pltpu.VMEM(el.shape, BF),
-            dma((4,)), dma((4,)), dma((4,)), dma((4,)), dma((3,)),
+            dma((4,)), dma((4,)), dma((2,)),
         ],
-        compiler_params=pltpu.CompilerParams(vmem_limit_bytes=60 * 1024 * 1024),
+        compiler_params=pltpu.CompilerParams(vmem_limit_bytes=40 * 1024 * 1024),
         name="physical",
     )(pre, last, ez, el)
     return out.reshape((1,) + out.shape)

time: 68.5 us -> 61.5 us (0.90)
  Pallas kernels: 68.1 us -> 61.3 us
    pallas_call x1, Pallas kernels: 62.2 us -> 58.1 us  [shards(): pl.pallas_call(spectral_kernel, out_shape=[pltpu.VMEM(field.shape, F32),...]
    pallas_call x1, Pallas kernels: 5.87 us -> 3.18 us  [shards(): pl.pallas_call(final_kernel, out_shape=jax.ShapeDtypeStruct(field.shape,...]
where the time goes in v3:
time: 61.5 us; the launch traced here: 61.3 us
  Pallas kernels  61.3 us (100%)
    pallas_call x1, Pallas kernels, shards(): pl.pallas_call(spectral_kernel, out_shape=[pltpu.VMEM(field.shape, F32),...  58.1 us
    pallas_call x1, Pallas kernels, shards(): pl.pallas_call(final_kernel, out_shape=jax.ShapeDtypeStruct(field.shape,...  3.18 us

profile of v3, /device:TPU:1, one launch (start us, length us, event | category | flops | bytes accessed | tf_op | source)
XLA Modules:
  0.0 61.3 jit_solution(11313094878127084933)
XLA Ops:
  0.0 58.1 %spectral.1 = (f32[48,8,16,256]{3,2,1,0:T(8,128)S(1)}, f32[16,64,128]{2,1,0:T(8,128)S(1)}) custom-call(f32[48,8,16,256]{3,2,1,0:T(8,128)} %bitcast.3, f32[2,4,32,2,2304]{4,3,2,1,0:T(2,128)} %weight.1, bf16[2,256,3072]{2,1,0:T(8,128)(2,1)} %constant.21.clone.spread, bf16[2304,128]{1,0:T(8,128)(2,1)} %constant.22.clone.gather, ...), custom_call_target="tpu_custom_call" | custom-call | tf_op jit(solution)/shard_map/spectral/pallas_call | solution.py:517
  58.1 3.2 %physical.1 = f32[48,8,16,256]{3,2,1,0:T(8,128)} custom-call(f32[48,8,16,256]{3,2,1,0:T(8,128)S(1)} %get-tuple-element.7.pre, f32[16,64,128]{2,1,0:T(8,128)S(1)} %get-tuple-element.8.modes, bf16[256,512]{1,0:T(8,128)(2,1)} %constant.25.clone.ez, bf16[128,512]{1,0:T(8,128)(2,1)} %constant.26.clone.el), custom_call_target="tpu_custom_call" | custom-call | tf_op jit(solution)/shard_map/physical/pallas_call | solution.py:528

commit v4 on v3

--- a/solution.py
+++ b/solution.py
@@ -132,6 +132,10 @@
     def field_copy(t):
         return pltpu.make_async_copy(field.at[pl.ds(t * 16, 16)], f_in.at[pl.ds(t * 16, 16)], f_sem.at[t])
 
+    def field_part(half):
+        at = (pl.ds(32, 16), pl.ds(half * 4, 4))
+        return pltpu.make_async_copy(field.at[at], f_in.at[at], f_sem.at[2 + half])
+
     def weight_copy(r, q):
         return pltpu.make_async_copy(weight.at[r, :, :, q, :], w_in.at[r, q], w_sem.at[r, q])
 
@@ -151,7 +155,9 @@
     ]
     first_table = pltpu.make_async_copy(tz_far, tz, c_sem.at[8])
     first_table.start()
-    for t in (2, 0, 1):
+    for half in range(2):
+        field_part(half).start()
+    for t in range(2):
         field_copy(t).start()
 
     barrier = pltpu.get_barrier_semaphore()
@@ -254,19 +260,20 @@
         return c
 
     first_table.wait()
-    field_copy(2).wait()
+    field_part(0).wait()
     z_both(0, 0)
     pl.semaphore_wait(barrier, G + H - 2)
     send1_all(TB, 0, 32)
     for copy in conv_copies:
         copy.start()
+    field_part(1).wait()
     z_both(1, 0)
     send1_all(TB, 32, 32)
     field_copy(0).wait()
     field_copy(1).wait()
     for half in range(2):
         lax.fori_loop(half * 2, half * 2 + 2, z_pair, 0)
-        send1_all(TA, half * 32, 32)
+    send1_all(TA, 0, 64)
     send1_all(TC, 0, 64)
     for t in range(CT):
         recv1[t, pl.ds(me * 64, 64), :] = send1[t, me]
@@ -361,8 +368,8 @@
             source, table = h_acc[...], r_in[768:, :]
         else:
             source, table = h_acc[:, (0 if t == TA else 768):(768 if t == TA else 1536)], r_in[:768, :]
-        high, low = split(source)
-        return dot(high, table) + dot(low, table)
+        both = dot(jnp.concatenate(split(source), axis=0), table)
+        return both[:128] + both[128:]
 
     def back_y(t):
         h_all = collect(t)
@@ -461,11 +468,12 @@
     give = [pltpu.make_async_copy(pre.at[pl.ds(8 * p, 8)], out.at[pl.ds(8 * p, 8)], o_sem.at[p]) for p in range(4)]
     for copy in small + give:
         copy.start()
-    for copy in small:
-        copy.wait()
     for p in range(4):
         tiles = [lanes16([modes[s, p * 16 + x * 8:p * 16 + (x + 1) * 8, :] for s in range(G)], lane) for x in range(2)]
         high, low = split(jnp.concatenate([tile[o] for o in range(16) for tile in tiles], axis=0))
+        if p == 0:
+            for copy in small:
+                copy.wait()
         spectral = dot(jnp.concatenate([high, low], axis=1), ez_in[...]) + dot(high, el_in[...])
         for h in range(2):
             y = slice(h * 8, (h + 1) * 8)
@@ -501,18 +509,18 @@
         pltpu.VMEM((384, 384), BF),
         pltpu.VMEM((384, 128), F32),
         pltpu.VMEM((CT, G, 64, 128), F32),
-        pltpu.VMEM((CT, G * 64, 128), F32),
-        pltpu.VMEM((CT, H * 32, 128), F32),
+        pltpu.VMEM((CT, G * 64 + 8, 128), F32),
+        pltpu.VMEM((CT, H * 32 + 8, 128), F32),
         pltpu.VMEM((CT, H * 32, 128), F32),
         pltpu.VMEM((CT, H, 32, 128), F32),
-        pltpu.VMEM((CT, H * 32, 128), F32),
-        pltpu.VMEM((CT, G * 64, 128), F32),
+        pltpu.VMEM((CT, H * 32 + 8, 128), F32),
+        pltpu.VMEM((CT, G * 64 + 8, 128), F32),
         pltpu.VMEM((2, G, 64, 128), F32),
         pltpu.VMEM((CT, 128, 3072), F32),
         pltpu.VMEM((128, 1536), F32),
     ]
     dma = pltpu.SemaphoreType.DMA
-    scratch += [dma((CT,)), dma((2, 2)), dma((11,))]
+    scratch += [dma((4,)), dma((2, 2)), dma((11,))]
     scratch += [dma((CT,))] * 8 + [dma]
     pre, last = pl.pallas_call(
         spectral_kernel,

time: 61.5 us -> 61.6 us (level)
  no operation moved by 1% of the time
where the time goes in v4:
time: 61.6 us; the launch traced here: 61.5 us
  Pallas kernels  61.4 us (100%)
    pallas_call x1, Pallas kernels, shards(): pl.pallas_call(spectral_kernel, out_shape=[pltpu.VMEM(field.shape, F32),...  58.2 us
    pallas_call x1, Pallas kernels, shards(): pl.pallas_call(final_kernel, out_shape=jax.ShapeDtypeStruct(field.shape,...  3.21 us

profile of v4, /device:TPU:1, one launch (start us, length us, event | category | flops | bytes accessed | tf_op | source)
XLA Modules:
  0.0 61.5 jit_solution(4470821511804626475)
XLA Ops:
  0.0 58.2 %spectral.1 = (f32[48,8,16,256]{3,2,1,0:T(8,128)S(1)}, f32[16,64,128]{2,1,0:T(8,128)S(1)}) custom-call(f32[48,8,16,256]{3,2,1,0:T(8,128)} %bitcast.3, f32[2,4,32,2,2304]{4,3,2,1,0:T(2,128)} %weight.1, bf16[2,256,3072]{2,1,0:T(8,128)(2,1)} %constant.21.clone.spread, bf16[2304,128]{1,0:T(8,128)(2,1)} %constant.22.clone.gather, ...), custom_call_target="tpu_custom_call" | custom-call | tf_op jit(solution)/shard_map/spectral/pallas_call | solution.py:525
  58.2 3.2 %physical.1 = f32[48,8,16,256]{3,2,1,0:T(8,128)} custom-call(f32[48,8,16,256]{3,2,1,0:T(8,128)S(1)} %get-tuple-element.7.pre, f32[16,64,128]{2,1,0:T(8,128)S(1)} %get-tuple-element.8.modes, bf16[256,512]{1,0:T(8,128)(2,1)} %constant.25.clone.ez, bf16[128,512]{1,0:T(8,128)(2,1)} %constant.26.clone.el), custom_call_target="tpu_custom_call" | custom-call | tf_op jit(solution)/shard_map/physical/pallas_call | solution.py:536

commit v5 on v4

--- a/solution.py
+++ b/solution.py
@@ -182,7 +182,7 @@
         def body(d, c):
             copy1(t, first_row, rows, lax.rem(me + d, G), me).start()
             return c
-        lax.fori_loop(1, G, body, 0)
+        lax.fori_loop(1, G, body, 0, unroll=True)
 
     def copy2(t, target, source):
         return pltpu.make_async_remote_copy(
@@ -209,7 +209,7 @@
         def body(d, c):
             copy(t, lax.rem(index + d, count), index).start()
             return c
-        lax.fori_loop(1, count, body, 0)
+        lax.fori_loop(1, count, body, 0, unroll=True)
 
     def all1(t):
         return pltpu.make_async_remote_copy(

time: 61.6 us -> 61.5 us (level)
  no operation moved by 1% of the time
where the time goes in v5:
time: 61.5 us; the launch traced here: 61.4 us
  Pallas kernels  61.4 us (100%)
    pallas_call x1, Pallas kernels, shards(): pl.pallas_call(spectral_kernel, out_shape=[pltpu.VMEM(field.shape, F32),...  58.2 us
    pallas_call x1, Pallas kernels, shards(): pl.pallas_call(final_kernel, out_shape=jax.ShapeDtypeStruct(field.shape,...  3.21 us

profile of v5, /device:TPU:1, one launch (start us, length us, event | category | flops | bytes accessed | tf_op | source)
XLA Modules:
  0.0 61.4 jit_solution(11085604628767104631)
XLA Ops:
  0.0 58.2 %spectral.1 = (f32[48,8,16,256]{3,2,1,0:T(8,128)S(1)}, f32[16,64,128]{2,1,0:T(8,128)S(1)}) custom-call(f32[48,8,16,256]{3,2,1,0:T(8,128)} %bitcast.3, f32[2,4,32,2,2304]{4,3,2,1,0:T(2,128)} %weight.1, bf16[2,256,3072]{2,1,0:T(8,128)(2,1)} %constant.21.clone.spread, bf16[2304,128]{1,0:T(8,128)(2,1)} %constant.22.clone.gather, ...), custom_call_target="tpu_custom_call" | custom-call | tf_op jit(solution)/shard_map/spectral/pallas_call | solution.py:525
  58.2 3.2 %physical.1 = f32[48,8,16,256]{3,2,1,0:T(8,128)} custom-call(f32[48,8,16,256]{3,2,1,0:T(8,128)S(1)} %get-tuple-element.7.pre, f32[16,64,128]{2,1,0:T(8,128)S(1)} %get-tuple-element.8.modes, bf16[256,512]{1,0:T(8,128)(2,1)} %constant.25.clone.ez, bf16[128,512]{1,0:T(8,128)(2,1)} %constant.26.clone.el), custom_call_target="tpu_custom_call" | custom-call | tf_op jit(solution)/shard_map/physical/pallas_call | solution.py:536

commit v6 on v4

--- a/solution.py
+++ b/solution.py
@@ -464,12 +464,12 @@
     lane = lax.broadcasted_iota(jnp.int32, (8, 128), 1)
     done = CH - 16
     small = [pltpu.make_async_copy(ez, ez_in, c_sem.at[0]), pltpu.make_async_copy(el, el_in, c_sem.at[1])]
-    store = [pltpu.make_async_copy(work.at[p], out.at[pl.ds(done, 16), pl.ds(2 * p, 2)], v_sem.at[p]) for p in range(4)]
+    store = [pltpu.make_async_copy(work.at[p], out.at[pl.ds(done, 16), pl.ds(4 * p, 4)], v_sem.at[p]) for p in range(2)]
     give = [pltpu.make_async_copy(pre.at[pl.ds(8 * p, 8)], out.at[pl.ds(8 * p, 8)], o_sem.at[p]) for p in range(4)]
     for copy in small + give:
         copy.start()
-    for p in range(4):
-        tiles = [lanes16([modes[s, p * 16 + x * 8:p * 16 + (x + 1) * 8, :] for s in range(G)], lane) for x in range(2)]
+    for p in range(2):
+        tiles = [lanes16([modes[s, p * 32 + x * 8:p * 32 + (x + 1) * 8, :] for s in range(G)], lane) for x in range(4)]
         high, low = split(jnp.concatenate([tile[o] for o in range(16) for tile in tiles], axis=0))
         if p == 0:
             for copy in small:
@@ -477,8 +477,8 @@
         spectral = dot(jnp.concatenate([high, low], axis=1), ez_in[...]) + dot(high, el_in[...])
         for h in range(2):
             y = slice(h * 8, (h + 1) * 8)
-            part = spectral[:, h * NZ:(h + 1) * NZ].reshape(16, 2, 8, NZ)
-            work[p, :, :, y, :] = gelu(pre[done:, 2 * p:2 * p + 2, y, :] + part)
+            part = spectral[:, h * NZ:(h + 1) * NZ].reshape(16, 4, 8, NZ)
+            work[p, :, :, y, :] = gelu(pre[done:, 4 * p:4 * p + 4, y, :] + part)
         store[p].start()
     for copy in store + give:
         copy.wait()
@@ -539,7 +539,7 @@
         in_specs=[VMEM, VMEM, ANY, ANY],
         out_specs=ANY,
         scratch_shapes=[
-            pltpu.VMEM((4, 16, 2, 16, NZ), F32),
+            pltpu.VMEM((2, 16, 4, 16, NZ), F32),
             pltpu.VMEM(ez.shape, BF),
             pltpu.VMEM(el.shape, BF),
             dma((4,)), dma((4,)), dma((2,)),

time: 61.6 us -> 61.5 us (level)
  no operation moved by 1% of the time
where the time goes in v6:
time: 61.5 us; the launch traced here: 61.4 us
  Pallas kernels  61.4 us (100%)
    pallas_call x1, Pallas kernels, shards(): pl.pallas_call(spectral_kernel, out_shape=[pltpu.VMEM(field.shape, F32),...  58.2 us
    pallas_call x1, Pallas kernels, shards(): pl.pallas_call(final_kernel, out_shape=jax.ShapeDtypeStruct(field.shape,...  3.15 us

profile of v6, /device:TPU:1, one launch (start us, length us, event | category | flops | bytes accessed | tf_op | source)
XLA Modules:
  0.0 61.4 jit_solution(13325693076953385818)
XLA Ops:
  0.0 58.2 %spectral.1 = (f32[48,8,16,256]{3,2,1,0:T(8,128)S(1)}, f32[16,64,128]{2,1,0:T(8,128)S(1)}) custom-call(f32[48,8,16,256]{3,2,1,0:T(8,128)} %bitcast.3, f32[2,4,32,2,2304]{4,3,2,1,0:T(2,128)} %weight.1, bf16[2,256,3072]{2,1,0:T(8,128)(2,1)} %constant.21.clone.spread, bf16[2304,128]{1,0:T(8,128)(2,1)} %constant.22.clone.gather, ...), custom_call_target="tpu_custom_call" | custom-call | tf_op jit(solution)/shard_map/spectral/pallas_call | solution.py:525
  58.2 3.1 %physical.1 = f32[48,8,16,256]{3,2,1,0:T(8,128)} custom-call(f32[48,8,16,256]{3,2,1,0:T(8,128)S(1)} %get-tuple-element.7.pre, f32[16,64,128]{2,1,0:T(8,128)S(1)} %get-tuple-element.8.modes, bf16[256,512]{1,0:T(8,128)(2,1)} %constant.25.clone.ez, bf16[128,512]{1,0:T(8,128)(2,1)} %constant.26.clone.el), custom_call_target="tpu_custom_call" | custom-call | tf_op jit(solution)/shard_map/physical/pallas_call | solution.py:536
